TPU v7x, 256 devices: a whole 4x4x8 slice. The times are simulated.
256 devices in a mesh: pole: 8 (over z_hi, core), row: 8 (over y, z_lo), col: 4 (over x).
Axes of the slice: x: 4, y: 4, z: 8 (z_hi: 4, z_lo: 2; z = z_hi * 2 + z_lo), core: 2. Of those that a mesh axis runs over, the one named last changes fastest.
Arguments:
- ancestor_inverse: bfloat16 [8, 6144, 6144], P('pole', 'row', 'col'), may hold values from -0.078125 to 0.078125
- factor_cols: bfloat16 [8, 6144, 4096], P('pole', None, ('row', 'col')), may hold values from -6 to 6
- diag_inverse: float32 [8, 4096], P('pole', ('row', 'col')), may hold values from 20 to 200
- pole_weights: float32 [8], P('pole'), may hold values from 0.004 to 0.02
- block_pattern: int32 [48, 32], replicated, may hold values 0 or 1
- supernode_ids: int32 [4096], replicated, may hold values from 0 to 31, never falling along the last dimension, each value on 1 to 2048 neighbouring positions
Outputs:
- inverse_block: bfloat16 [8, 6144, 8, 4, 128], P('pole', 'row', None, 'col')
- density_diag: float32 [4096], P(('row', 'col'))
Inputs may be any that keep to these rules, and one draw needn't show every extreme that they name: `supernode_ids`: never falling along the columns; each supernode has 1 to 2048 columns, one exactly 2048.
All inputs are finite; a program needn't handle non-finite values.
Results may differ from a plain program's by a relative error of at most 0.001.
Values may be sent and summed in bfloat16 or wider, within the bound.
A program may use at most 192 MiB of HBM per device.

v0:
```python
import jax
import jax.numpy as jnp
from jax import lax
from jax.sharding import PartitionSpec as P

RBLK = 128


def column_mask(block_pattern, col_ids, first_block, block_count):
    pattern_rows = lax.dynamic_slice_in_dim(block_pattern, first_block, block_count, 0).astype(
        jnp.float32
    )
    onehot = (
        col_ids[None, :] == jnp.arange(block_pattern.shape[1], dtype=jnp.int32)[:, None]
    ).astype(jnp.float32)
    coarse = jnp.dot(pattern_rows, onehot, precision=lax.Precision.HIGHEST)
    return jnp.repeat(coarse, RBLK, axis=0).astype(jnp.bfloat16)


def per_device(
    ancestor_inverse, factor_cols, diag_inverse, pole_weights, block_pattern, supernode_ids
):
    row_devices = lax.axis_size("row")
    col_devices = lax.axis_size("col")
    row_index = lax.axis_index("row")
    col_index = lax.axis_index("col")
    block_cols = factor_cols.shape[2]
    matrix_rows = factor_cols.shape[1]
    row_span = matrix_rows // row_devices
    ids_grid = supernode_ids.reshape(row_devices, col_devices, block_cols)
    own_ids = lax.dynamic_index_in_dim(ids_grid, col_index, 1, keepdims=False).reshape(-1)
    col_span = matrix_rows // col_devices
    parted = lax.all_to_all(factor_cols, "col", split_axis=1, concat_axis=2, tiled=True)
    parted = parted.reshape(col_span, col_devices, 1, block_cols)
    gathered = lax.all_gather(parted, "row", axis=2, tiled=True).reshape(col_span, -1)
    all_ids = jnp.transpose(ids_grid, (1, 0, 2)).reshape(-1)
    masked = gathered * column_mask(
        block_pattern, all_ids, col_index * (col_span // RBLK), col_span // RBLK
    )
    partial_value = jnp.dot(ancestor_inverse[0], masked, preferred_element_type=jnp.float32)
    product = lax.psum_scatter(partial_value, "col", scatter_dimension=1, tiled=True)
    own_part = lax.all_to_all(factor_cols, "row", split_axis=1, concat_axis=2, tiled=True)
    own_rows = own_part[0] * column_mask(
        block_pattern, own_ids, row_index * (row_span // RBLK), row_span // RBLK
    )
    inner_sums = jnp.sum(own_rows.astype(jnp.float32) * product, axis=0)
    inverse_block = (-product).astype(jnp.bfloat16).reshape(1, row_span, row_devices, 1, block_cols)
    pole_weight = pole_weights[0]
    row_total = lax.psum_scatter(inner_sums, "row", scatter_dimension=0, tiled=True)
    weighted = pole_weight * (diag_inverse[0] + row_total)
    density_diag = lax.psum(weighted, "pole")
    return (inverse_block, density_diag)


def solution(mesh):
    in_specs = (
        P("pole", "row", "col"),
        P("pole", None, ("row", "col")),
        P("pole", ("row", "col")),
        P("pole"),
        P(),
        P(),
    )
    out_specs = (P("pole", "row", None, "col", None), P(("row", "col")))
    return jax.shard_map(
        per_device, mesh=mesh, in_specs=in_specs, out_specs=out_specs, check_vma=False
    )
```

profile of v0, /device:TPU:1, one launch (start us, length us, event | category | flops | bytes accessed | tf_op | source)
XLA Modules:
  0.0 551.8 jit_solution(9412325891938649768)
XLA Ops:
  7.2 6.1 %copy.48 = bf16[1,6144,128]{2,0,1:T(2,128)(2,1)} copy(bf16[1,6144,128]{2,1,0:T(8,128)(2,1)} %param.7) | data formatting | bytes 3145728 | tf_op args[1]
  13.8 35.4 %reduce = bf16[6144,128]{1,0:T(8,128)(2,1)} reduce(bf16[6144,1,128]{2,1,0:T(2,128)(2,1)} %bitcast.57, bf16[]{:T(256)} %broadcast.2), dimensions={1}, to_apply=%bitcast.48.reduce_sub_computation | reduce | bytes 3145730
  49.2 3.7 reshape.30
  53.0 22.8 %all_to_all.30 = bf16[4,2,98304]{2,1,0:T(2,128)(2,1)} all-to-all(bf16[4,2,98304]{2,1,0:T(2,128)(2,1)} %reshape.30), channel_id=1, replica_groups=mesh['pole'=8,'row'=8,'col'=4] {'col'}, dimensions={0} | all-to-all | bytes 3145728 | tf_op jit(solution)/shard_map/all_to_all | solution.py:33
  75.8 4.5 reshape.31
  80.3 3.3 copy.38
  84.2 6.2 %broadcast_in_dim.8 = bf16[12,128,4096]{2,1,0:T(8,128)(2,1)} broadcast(bf16[12,4096]{1,0:T(8,128)(2,1)S(1)} %convolution_convert_fusion), dimensions={0,2} | broadcast | bytes 12681216 | tf_op jit(solution)/shard_map/broadcast_in_dim | solution.py:17
  90.4 11.5 %copy.41 = bf16[192,8,32,128]{3,2,1,0:T(8,128)(2,1)} copy(bf16[192,8,32,128]{3,1,2,0:T(8,128)(2,1)} %bitcast.50) | data formatting | bytes 25165824
  101.9 235.7 %all-gather.3.cloned.1.call-done = bf16[1,1536,4,1024]{3,1,2,0:T(8,128)(2,1)} async-done(((bf16[1,1536,4,128]{3,1,2,0:T(8,128)(2,1)}), bf16[1,1536,4,1024]{3,1,2,0:T(8,128)(2,1)}) %all-gather.3.cloned.1.call-update) | async-done | bytes 12582928 | tf_op jit(solution)/shard_map/all_gather | solution.py:35
  337.6 9.1 %copy.40 = bf16[768,8,8,128]{3,2,1,0:T(8,128)(2,1)S(1)} copy(bf16[768,8,8,128]{3,1,2,0:T(8,128)(2,1)} %bitcast.55) | data formatting | bytes 25165824
  346.7 5.5 copy_multiply_fusion
  352.2 16.7 %copy.33 = bf16[1536,4,8,128]{0,3,2,1:T(8,128)(2,1)} copy(bf16[1536,4,8,128]{3,2,1,0:T(8,128)(2,1)} %copy_multiply_fusion) | data formatting | bytes 25165824 | tf_op jit(solution)/shard_map/mul | solution.py:37
  368.9 15.6 %convolution_bitcast_fusion = f32[768,4096]{0,1:T(8,128)} fusion(bf16[1536,4096]{0,1:T(8,128)(2,1)} %bitcast.56, bf16[1,768,1536]{2,1,0:T(8,128)(2,1)S(1)} %copy-done), kind=kOutput, calls=%fused_computation.1 | convolution fusion | flops 9663676416 | bytes 27525120 | tf_op jit(solution)/shard_map/dot_general | solution.py:40
  385.9 25.1 %copy.47 = bf16[1,6144,128]{2,0,1:T(2,128)(2,1)} copy(bf16[1,6144,128]{2,1,0:T(8,128)(2,1)S(1)} %copy-done.2) | data formatting | bytes 3145728 | tf_op args[1]
  411.1 34.5 %reduce.1 = bf16[6144,128]{1,0:T(8,128)(2,1)S(1)} reduce(bf16[6144,1,128]{2,1,0:T(2,128)(2,1)} %bitcast.59, bf16[]{:T(256)} %broadcast.2), dimensions={1}, to_apply=%bitcast.47.reduce_sub_computation | reduce | bytes 3145730
  447.5 4.6 all-to-all-start.1
  456.0 16.6 %all-to-all-done.1 = bf16[8,2,49152]{2,1,0:T(2,128)(2,1)} async-done(((bf16[8,2,49152]{2,1,0:T(2,128)(2,1)}), bf16[8,2,49152]{2,1,0:T(2,128)(2,1)}, u32[]{:S(2)}, u32[]{:S(2)}) %all-to-all-start.1) | async-done | bytes 1572896 | tf_op jit(solution)/shard_map/all_to_all | solution.py:42
  472.6 6.4 %reshape.33 = bf16[6144,1,128]{2,1,0:T(2,128)(2,1)} reshape(bf16[8,2,49152]{2,1,0:T(2,128)(2,1)} %all-to-all-done.1) | data formatting | bytes 3145728
  478.9 2.1 copy.39
  482.6 20.1 %reduce-scatter.2.cloned.1.call-done = f32[768,1024]{0,1:T(8,128)} async-done(((f32[768,4096]{0,1:T(8,128)}), f32[768,1024]{0,1:T(8,128)}) %reduce-scatter.2.cloned.1.call-update) | async-done | bytes 3145744 | tf_op jit(solution)/shard_map/reduce_scatter | solution.py:41
  502.7 4.8 multiply_reduce_fusion
  507.5 2.9 copy.37
  510.5 16.0 %all-reduce = f32[1024]{0:T(1024)S(1)} all-reduce(f32[1024]{0:T(1024)S(1)} %get-tuple-element.12), channel_id=4, replica_groups=mesh['pole'=8,'row'=8,'col'=4] {'row'}, use_global_device_ids=true, to_apply=%region_2.3.clone | all-reduce | flops 1024 | bytes 8192
  526.5 18.4 %psum.7 = f32[128]{0:T(128)} all-reduce(f32[128]{0:T(128)S(1)} %fusion.9), channel_id=1, replica_groups=mesh['pole'=8,'row'=8,'col'=4] {'pole'}, use_global_device_ids=true, to_apply=%region_3.4 | all-reduce | flops 128 | bytes 1024 | tf_op jit(solution)/shard_map/psum | solution.py:51
  (36 shorter events, 8.8 us)
Async XLA Ops:
  7.2 361.7 %copy-start = (bf16[1,768,1536]{2,1,0:T(8,128)(2,1)S(1)}, bf16[1,768,1536]{2,1,0:T(8,128)(2,1)}, u32[]{:S(2)}) copy-start(bf16[1,768,1536]{2,1,0:T(8,128)(2,1)} %param.6) | copy-start | bytes 7077892
  7.2 330.4 %all-gather.3.cloned.1.call-start = ((), (), s32[]{:S(2)}) async-start(), calls=%async_computation.4 | async-start | bytes 14155776 | tf_op jit(solution)/shard_map/all_gather | solution.py:35
  80.3 3.5 copy-start.4
  80.3 3.5 copy-start.3
  83.5 419.2 %reduce-scatter.2.cloned.1.call-start = ((), (), s32[]{:S(2)}) async-start(), calls=%async_computation.3 | async-start | bytes 15728640 | tf_op jit(solution)/shard_map/reduce_scatter | solution.py:41
  337.6 9.1 %slice-start = ((s8[12582912]{0:T(1024)(128)(4,1)}), s8[4194304]{0:T(1024)(128)(4,1)S(1)}, s32[]{:S(2)}) async-start(s8[12582912]{0:T(1024)(128)(4,1)} %bitcast.51), calls=%async_computation.5 | async-start | bytes 8388608
  337.6 9.1 %slice-start.1 = ((s8[12582912]{0:T(1024)(128)(4,1)}), s8[4194304]{0:T(1024)(128)(4,1)S(1)}, s32[]{:S(2)}) async-start(s8[12582912]{0:T(1024)(128)(4,1)} %bitcast.51), calls=%async_computation.6 | async-start | bytes 8388608
  337.6 9.1 %slice-start.2 = ((s8[12582912]{0:T(1024)(128)(4,1)}), s8[4194304]{0:T(1024)(128)(4,1)S(1)}, s32[]{:S(2)}) async-start(s8[12582912]{0:T(1024)(128)(4,1)} %bitcast.51), calls=%async_computation.7 | async-start | bytes 8388608
  384.5 1.4 copy-start.2
  447.5 25.1 %all-to-all-start.1 = ((bf16[8,2,49152]{2,1,0:T(2,128)(2,1)}), bf16[8,2,49152]{2,1,0:T(2,128)(2,1)}, u32[]{:S(2)}, u32[]{:S(2)}) async-start(bf16[8,2,49152]{2,1,0:T(2,128)(2,1)} %reshape.32), calls=%async_computation.2 | async-start | bytes 3145728 | tf_op jit(solution)/shard_map/all_to_all | solution.py:42
  452.0 2.7 copy-start.6
  502.7 42.2 %copy-start.1 = (bf16[1,768,1536]{2,1,0:T(8,128)(2,1)S(1)}, bf16[1,768,1536]{2,1,0:T(8,128)(2,1)}, u32[]{:S(2)}) copy-start(bf16[1,768,1536]{2,1,0:T(8,128)(2,1)} %param.6) | copy-start | bytes 7077892
  507.5 18.9 %copy-start.5 = (f32[1,128]{1,0:T(1,128)S(1)}, f32[1,128]{1,0:T(1,128)}, u32[]{:S(2)}) copy-start(f32[1,128]{1,0:T(1,128)} %param.8) | copy-start | bytes 1540
Sparse Core Ops, SparseCore 0:
  83.7 253.8 all-gather.2
  384.7 118.0 reduce-scatter.1
where the time goes:
time: 553 us; the launch traced here: 552 us
  waiting for transfers between devices  272 us (49%)
  local copies, waits for them, and re-layouts  105 us (19%)
  other arithmetic  80.3 us (15%)
  blocking collectives  57.2 us (10%)
  matrix products  16.3 us (3%)
  between operations  15.5 us (3%)
    all_gather x1, waiting for transfers between devices, per_device(): lax.all_gather(parted, 'row', axis=2, tiled=True).reshape(col_span, -1)  236 us
    unnamed x33, local copies, waits for them, and re-layouts  79 us
    unnamed x3, other arithmetic  70 us
    all_to_all x1, blocking collectives, per_device(): lax.all_to_all(factor_cols, 'col', split_axis=1, concat_axis=2, tiled=True)  22.8 us
    reduce_scatter x1, waiting for transfers between devices, per_device(): lax.psum_scatter(partial_value, 'col', scatter_dimension=1, tiled=True)  20.1 us
    psum x1, blocking collectives, per_device(): density_diag = lax.psum(weighted, 'pole')  18.4 us
    mul x1, local copies, waits for them, and re-layouts, per_device(): gathered * column_mask(block_pattern, all_ids, col_index * (col_span // R...  16.7 us
    all_to_all x1, waiting for transfers between devices, per_device(): lax.all_to_all(factor_cols, 'row', split_axis=1, concat_axis=2, tiled=True)  16.6 us
  transfers between devices with their start and end apart: 3, of which 3 were waited for; matrix products, arithmetic and copies ran while one was open for 17% of the time, Pallas kernels for 0%

commit v1 on v0

v1 whole, which is shorter than its diff:
```python
import functools

import jax
import jax.numpy as jnp
from jax import lax
from jax.experimental import pallas as pl
from jax.experimental.pallas import tpu as pltpu
from jax.sharding import PartitionSpec as P

MESH = pl.DeviceIdType.MESH
F32, BF16 = jnp.float32, jnp.bfloat16

UNITS = 24
SLOTS = [(dy, dz) for dy in range(4) for dz in range(2)]
OWN, ZP, YN, YP, YF = (0, 0), (0, 1), (1, 0), (3, 0), (2, 0)
YNZ, YPZ, YFZ = (1, 1), (3, 1), (2, 1)
PAIRS = [(OWN, ZP), (YN, YP), (YNZ, YPZ), (YF, YFZ)]

QUARTER = [(0, 6), (6, 6), (12, 6), (18, 6)]
Y_UP = (
    [(OWN, YP, s, n) for s, n in QUARTER]
    + [(YP, YF, 0, 6), (YP, YF, 6, 6)]
    + [(ZP, YPZ, 0, 6), (ZP, YPZ, 6, 6), (ZP, YPZ, 12, 2)]
    + [(YPZ, YFZ, 0, 4), (YPZ, YFZ, 4, 2)]
)
Y_DOWN = (
    [(OWN, YN, s, n) for s, n in QUARTER[2:] + QUARTER[:2]]
    + [(YN, YF, 12, 6), (YN, YF, 18, 6)]
    + [(ZP, YNZ, 6, 6), (ZP, YNZ, 0, 6), (ZP, YNZ, 12, 2)]
    + [(YNZ, YFZ, 6, 4), (YNZ, YFZ, 10, 2)]
)
Z_SWAP = (
    [(OWN, ZP, s, n) for s, n in QUARTER]
    + [(YN, YNZ, 14, 10), (YP, YPZ, 14, 10)]
    + [(YF, YFZ, 12, 6), (YF, YFZ, 18, 4), (YF, YFZ, 22, 2)]
)
X_UP = [(0, 3, m) for m in (0, 1, 2, 3, 4, 5)] + [(3, 2, m) for m in (0, 1, 2)]
X_DOWN = [(0, 1, m) for m in (3, 4, 5, 0, 1, 2)] + [(1, 2, m) for m in (3, 4, 5)]


def at_slot(slot):
    return slot[0] * 2 + slot[1]


def kernel(
    a_hbm, f_hbm, diag_ref, weight_ref, pattern_ref, ids_ref,
    out_hbm, density_ref,
    a_all, f_all, acc, coarse, out_vmem, part, red, pol,
    load_sem, out_sem, f_send, f_recv, a_send, a_recv, red_send, red_recv, pol_send, pol_recv,
):
    pole, row, col = lax.axis_index("pole"), lax.axis_index("row"), lax.axis_index("col")
    n_pole = lax.axis_size("pole")
    y, z = row // 2, row % 2
    rows, depth = a_all.shape[1], a_all.shape[2]
    unit, sixth = f_all.shape[1] // UNITS, rows // 6
    blocks = coarse.shape[0] // 4
    rblk = depth // blocks

    def row_of(slot):
        return ((y + slot[0]) % 4) * 2 + (z + slot[1]) % 2

    x_up, x_down = {"col": (col + 1) % 4}, {"col": (col + 3) % 4}
    y_up, y_down, z_swap = {"row": row_of(YN)}, {"row": row_of(YP)}, {"row": row_of(ZP)}

    own_rows = pltpu.make_async_copy(a_hbm.at[0], a_all.at[0], load_sem.at[4])
    loads = []
    for q in range(4):
        source = pl.ds(pl.multiple_of(((col + q) % 4) * depth, depth), depth)
        loads.append(
            pltpu.make_async_copy(f_hbm.at[0, source], f_all.at[0, pl.ds(q * depth, depth)], load_sem.at[q])
        )
    for load in loads:
        load.start()
    own_rows.start()

    barrier = pltpu.get_barrier_semaphore()
    friends = [x_up, x_down]
    friends += [{"row": row_of(slot)} for slot in SLOTS[1:]]
    friends += [{"pole": (pole + d) % n_pole} for d in range(1, n_pole)]
    for friend in friends:
        pl.semaphore_signal(barrier, inc=1, device_id=friend, device_id_type=MESH)
    pl.semaphore_wait(barrier, len(friends))

    def f_copies(link, plan, device):
        copies = []
        for i, (here, there, first, count) in enumerate(plan):
            span = pl.ds(first * unit, count * unit)
            copies.append(
                pltpu.make_async_remote_copy(
                    src_ref=f_all.at[at_slot(here), span],
                    dst_ref=f_all.at[at_slot(there), span],
                    send_sem=f_send.at[link, i],
                    recv_sem=f_recv.at[link, i],
                    device_id=device,
                    device_id_type=MESH,
                )
            )
        return copies

    def a_copies(link, plan, device):
        copies = []
        for i, (here, there, m) in enumerate(plan):
            span = pl.ds(m * sixth, sixth)
            copies.append(
                pltpu.make_async_remote_copy(
                    src_ref=a_hbm.at[0, span] if here == 0 else a_all.at[here, span],
                    dst_ref=a_all.at[there, span],
                    send_sem=a_send.at[link, i],
                    recv_sem=a_recv.at[link, i],
                    device_id=device,
                    device_id_type=MESH,
                )
            )
        return copies

    yu, yd, zs = f_copies(0, Y_UP, y_up), f_copies(1, Y_DOWN, y_down), f_copies(2, Z_SWAP, z_swap)
    xu, xd = a_copies(0, X_UP, x_up), a_copies(1, X_DOWN, x_down)

    def start(copies, *which):
        for i in which:
            copies[i].start()

    def arrived(copies, *which):
        for i in which:
            copies[i].wait_recv()

    start(xu, 0)
    start(xd, 0)

    ids = ids_ref[pl.ds(row * 4 + col, 1), :]
    onehot = jnp.where(ids == lax.broadcasted_iota(jnp.int32, (pattern_ref.shape[0], ids.shape[1]), 0), 1.0, 0.0)
    coarse[...] = lax.dot_general(
        pattern_ref[...].astype(F32).astype(BF16), onehot.astype(BF16), (((0,), (0,)), ((), ())),
        preferred_element_type=F32,
    )

    def mask_quarter(q):
        loads[q].wait()
        first = ((col + q) % 4) * blocks

        def body(j, carry):
            span = pl.ds(pl.multiple_of(q * depth + j * rblk, rblk), rblk)
            mask = coarse[pl.ds(first + j, 1), :].astype(BF16)
            f_all[0, span, :] = f_all[0, span, :] * mask
            return carry

        lax.fori_loop(0, blocks, body, 0)

    mask_quarter(0)
    start(yu, 0)
    start(zs, 0)
    mask_quarter(2)
    start(yd, 0)
    mask_quarter(1)
    start(yu, 1)
    start(zs, 1)
    start(xu, 1)
    start(xd, 1)
    mask_quarter(3)
    start(yd, 1)
    start(yu, 2)
    start(zs, 2)
    start(yd, 2)
    start(xu, 2)
    start(xd, 2)
    start(yu, 3)
    start(zs, 3)
    start(yd, 3)
    start(xu, 3, 4, 5)
    start(xd, 3, 4, 5)

    def multiply(pair, q):
        span = slice(q * depth, (q + 1) * depth)
        right = jnp.concatenate([f_all[at_slot(s), span, :] for s in PAIRS[pair]], axis=1)
        product = jnp.dot(a_all[q], right, preferred_element_type=F32)
        if q == 0:
            acc[pair] = product
        else:
            acc[pair] = acc[pair] + product

    own_span = pl.ds(pl.multiple_of(((row * rows // depth - col + 4) % 4) * depth + (row * rows) % depth, rows), rows)
    outs, reds = [], []

    def finish(pair):
        for half, slot in enumerate(PAIRS[pair]):
            s = at_slot(slot)
            product = acc[pair, :, half * 128 : (half + 1) * 128]
            out_vmem[s] = (-product).astype(BF16)
            columns = pl.ds(pl.multiple_of(row_of(slot) * 128, 128), 128)
            outs.append(pltpu.make_async_copy(out_vmem.at[s], out_hbm.at[:, columns], out_sem.at[s]))
            outs[-1].start()
            terms = f_all[s, own_span, :].astype(F32) * product
            sums = jnp.sum(terms.reshape(rows // 8, 8, 128), axis=0)
            if slot == OWN:
                red[0] = sums
                continue
            part[s] = sums
            back = at_slot(((-slot[0]) % 4, slot[1]))
            copy = pltpu.make_async_remote_copy(
                src_ref=part.at[s],
                dst_ref=red.at[back],
                send_sem=red_send.at[s],
                recv_sem=red_recv.at[back],
                device_id={"row": row_of(slot)},
                device_id_type=MESH,
            )
            copy.start()
            reds.append(copy)

    own_rows.wait()
    arrived(zs, 0)
    multiply(0, 0)
    arrived(yu, 0, 1)
    start(yu, 4, 5)
    arrived(yd, 0, 1)
    start(yd, 4, 5)
    arrived(xu, 0, 1, 2)
    start(xu, 6, 7, 8)
    arrived(xd, 0, 1, 2)
    start(xd, 6, 7, 8)
    arrived(zs, 1, 2, 3)
    start(yu, 6, 7, 8)
    start(yd, 6, 7, 8)
    arrived(yu, 2, 3)
    arrived(yd, 2, 3)
    start(zs, 4, 5)
    multiply(1, 0)
    arrived(yu, 4, 5)
    arrived(yd, 4, 5)
    start(zs, 6, 7, 8)
    arrived(xu, 3, 4, 5)
    arrived(xd, 3, 4, 5)
    multiply(0, 1)
    multiply(0, 3)
    arrived(yu, 6)
    start(yu, 9, 10)
    arrived(yd, 6)
    start(yd, 9, 10)
    multiply(1, 1)
    multiply(1, 3)
    arrived(zs, 4, 5)
    arrived(yu, 7, 8)
    arrived(yd, 7, 8)
    multiply(2, 0)
    multiply(2, 1)
    multiply(2, 3)
    arrived(xu, 6, 7, 8)
    arrived(xd, 6, 7, 8)
    for pair in range(3):
        multiply(pair, 2)
        finish(pair)
    arrived(yu, 9, 10)
    arrived(yd, 9, 10)
    arrived(zs, 6, 7, 8)
    for q in range(4):
        multiply(3, q)
    finish(3)

    for copy in reds:
        copy.wait_recv()
    total = red[0]
    for s in range(1, 8):
        total = total + red[s]
    inner = jnp.sum(total, axis=0, keepdims=True)
    weighted = weight_ref[0] * (diag_ref[...] + inner)
    pol[pole] = jnp.broadcast_to(weighted, pol.shape[1:])
    pols = []
    for d in range(1, n_pole):
        copy = pltpu.make_async_remote_copy(
            src_ref=pol.at[pole],
            dst_ref=pol.at[pole],
            send_sem=pol_send.at[d],
            recv_sem=pol_recv.at[d],
            device_id={"pole": (pole + d) % n_pole},
            device_id_type=MESH,
        )
        copy.start()
        pols.append(copy)
    for copy in pols:
        copy.wait_recv()
    density = pol[0]
    for p in range(1, n_pole):
        density = density + pol[p]
    density_ref[...] = density[:1]

    for copies in (yu, yd, zs, xu, xd, reds, pols):
        for copy in copies:
            copy.wait_send()
    for copy in outs:
        copy.wait()


def per_device(ancestor_inverse, factor_cols, diag_inverse, pole_weights, block_pattern, supernode_ids):
    _, rows, depth = ancestor_inverse.shape
    _, height, width = factor_cols.shape
    blocks = block_pattern.shape[0]
    vmem = pl.BlockSpec(memory_space=pltpu.VMEM)
    anywhere = pl.BlockSpec(memory_space=pl.ANY)
    dma = pltpu.SemaphoreType.DMA
    links = max(len(Y_UP), len(Z_SWAP))
    out, density = pl.pallas_call(
        kernel,
        out_shape=(
            jax.ShapeDtypeStruct((rows, 8 * width), BF16),
            jax.ShapeDtypeStruct((1, width), F32),
        ),
        in_specs=[anywhere, anywhere, vmem, pl.BlockSpec(memory_space=pltpu.SMEM), vmem, vmem],
        out_specs=(anywhere, vmem),
        scratch_shapes=[
            pltpu.VMEM((4, rows, depth), BF16),
            pltpu.VMEM((8, height, width), BF16),
            pltpu.VMEM((4, rows, 2 * width), F32),
            pltpu.VMEM((blocks, width), F32),
            pltpu.VMEM((8, rows, width), BF16),
            pltpu.VMEM((8, 8, width), F32),
            pltpu.VMEM((8, 8, width), F32),
            pltpu.VMEM((8, 8, width), F32),
            dma((5,)),
            dma((8,)),
            dma((3, links)),
            dma((3, links)),
            dma((2, len(X_UP))),
            dma((2, len(X_UP))),
            dma((8,)),
            dma((8,)),
            dma((8,)),
            dma((8,)),
        ],
        compiler_params=pltpu.CompilerParams(
            collective_id=0, has_side_effects=True, vmem_limit_bytes=56 * 1024 * 1024
        ),
        cost_estimate=pl.CostEstimate(
            flops=2 * rows * height * 8 * width, bytes_accessed=6 * 1024 * 1024, transcendentals=0
        ),
    )(
        ancestor_inverse,
        factor_cols,
        diag_inverse,
        pole_weights,
        block_pattern.T,
        supernode_ids.reshape(-1, width),
    )
    return out.reshape(1, rows, 8, 1, width), density.reshape(width)


def solution(mesh):
    in_specs = (
        P("pole", "row", "col"),
        P("pole", None, ("row", "col")),
        P("pole", ("row", "col")),
        P("pole"),
        P(),
        P(),
    )
    out_specs = (P("pole", "row", None, "col", None), P(("row", "col")))
    return jax.shard_map(per_device, mesh=mesh, in_specs=in_specs, out_specs=out_specs, check_vma=False)
```

time: 553 us -> 114 us (0.21)
  waiting for transfers between devices: 272 us -> 0 us
  Pallas kernels: 0 us -> 109 us
  local copies, waits for them, and re-layouts: 105 us -> 3.52 us
  other arithmetic: 80.3 us -> 0 us
  blocking collectives: 57.2 us -> 0 us
  matrix products: 16.3 us -> 0 us
  between operations: 15.5 us -> 1.29 us
    all_gather x1 -> x0, waiting for transfers between devices: 236 us -> none  [per_device(): lax.all_gather(parted, 'row', axis=2, tiled=True).reshape(col_span, -1)]
    pallas_call x0 -> x1, Pallas kernels: none -> 109 us  [per_device(): pl.pallas_call(kernel, out_shape=(jax.ShapeDtypeStruct((rows, 8 * width),...]
    unnamed x33 -> x4, local copies, waits for them, and re-layouts: 79 us -> 3.52 us
    unnamed x3 -> x0, other arithmetic: 70 us -> none
    all_to_all x1 -> x0, blocking collectives: 22.8 us -> none  [per_device(): lax.all_to_all(factor_cols, 'col', split_axis=1, concat_axis=2, tiled=True)]
    reduce_scatter x1 -> x0, waiting for transfers between devices: 20.1 us -> none  [per_device(): lax.psum_scatter(partial_value, 'col', scatter_dimension=1, tiled=True)]
    psum x1 -> x0, blocking collectives: 18.4 us -> none  [per_device(): density_diag = lax.psum(weighted, 'pole')]
    mul x1 -> x0, local copies, waits for them, and re-layouts: 16.7 us -> none  [per_device(): gathered * column_mask(block_pattern, all_ids, col_index * (col_span // R...]
  transfers between devices with their start and end apart: 3 -> 0, of which waited for: 3 -> 0; matrix products, arithmetic and copies ran while one was open for 17% -> 0% of each run, Pallas kernels for 0% -> 0%
where the time goes in v1:
time: 114 us
  Pallas kernels  109 us (96%)
  local copies, waits for them, and re-layouts  3.52 us (3%)
  between operations  1.29 us (1%)
    pallas_call x1, Pallas kernels, per_device(): pl.pallas_call(kernel, out_shape=(jax.ShapeDtypeStruct((rows, 8 * width),...  109 us
    unnamed x4, local copies, waits for them, and re-layouts  3.52 us

profile of v1, /device:TPU:1, one launch (start us, length us, event | category | flops | bytes accessed | tf_op | source)
XLA Modules:
  0.0 113.6 jit_solution(10065499730209016699)
XLA Ops:
  1.3 108.8 %shard_map.77 = (bf16[768,1024]{1,0:T(8,128)(2,1)}, f32[1,128]{1,0:T(1,128)}) custom-call(bf16[1,768,1536]{2,1,0:T(8,128)(2,1)} %a_hbm.1, bf16[1,6144,128]{2,1,0:T(8,128)(2,1)} %f_hbm.1, f32[1,128]{1,0:T(1,128)} %diag_ref.1, f32[1]{0:T(128)S(6)} %copy.11.weight_ref, s32[32,48]{1,0:T(8,128)} %bitcast.11, s32[32,128]{1,0:T(8,128)} %bitcast.12), custom_call_target="tpu_custom_call" | custom-call | flops 9663676416 | bytes 6291456 | tf_op jit(solution)/shard_map/pallas_call | solution.py:301
  110.1 0.0 copy-start
  110.1 3.0 %copy.9 = bf16[96,8,8,128]{3,2,1,0:T(8,128)(2,1)} copy(bf16[96,8,8,128]{3,1,2,0:T(8,128)(2,1)} %bitcast.10) | data formatting | bytes 3145728
  113.1 0.0 copy-done
  113.1 0.5 copy.12
Async XLA Ops:
  110.1 3.0 %copy-start = (f32[1,128]{1,0:T(1,128)S(1)}, f32[1,128]{1,0:T(1,128)}, u32[]{:S(2)}) copy-start(f32[1,128]{1,0:T(1,128)} %get-tuple-element.5) | copy-start | bytes 1540

commit v2 on v1

v2 whole, which is shorter than its diff:
```python
import functools

import jax
import jax.numpy as jnp
from jax import lax
from jax.experimental import pallas as pl
from jax.experimental.pallas import tpu as pltpu
from jax.sharding import PartitionSpec as P

MESH = pl.DeviceIdType.MESH
F32, BF16 = jnp.float32, jnp.bfloat16

UNITS = 24
OWN, ZP, YN, YP = (0, 0), (0, 1), (1, 0), (3, 0)
YNZ, YPZ, YF, YFZ = (1, 1), (3, 1), (2, 0), (2, 1)
SLOTS = [OWN, ZP, YN, YP, YNZ, YPZ, YF, YFZ]

Y_UP = [
    (OWN, YP, 0, 6), (OWN, YP, 6, 6), (OWN, YP, 14, 10),
    (YP, YF, 0, 6), (YP, YF, 6, 6),
    (ZP, YPZ, 0, 6), (ZP, YPZ, 6, 6), (ZP, YPZ, 12, 2),
    (YPZ, YFZ, 0, 3), (YPZ, YFZ, 3, 3),
    (OWN, YP, 12, 2),
]
Y_DOWN = [
    (OWN, YN, 12, 6), (OWN, YN, 18, 6), (OWN, YN, 0, 10),
    (YN, YF, 12, 6), (YN, YF, 18, 6),
    (ZP, YNZ, 6, 6), (ZP, YNZ, 0, 6), (ZP, YNZ, 12, 2),
    (YNZ, YFZ, 6, 3), (YNZ, YFZ, 9, 3),
    (OWN, YN, 10, 2),
]
Z_SWAP = [
    (OWN, ZP, 0, 6), (OWN, ZP, 6, 6), (OWN, ZP, 12, 6), (OWN, ZP, 18, 4),
    (YN, YNZ, 14, 10), (YP, YPZ, 14, 10),
    (YF, YFZ, 12, 6), (YF, YFZ, 18, 3), (YF, YFZ, 21, 3),
    (OWN, ZP, 22, 2),
]
X_UP = [(0, 3, m) for m in (0, 2, 4, 1, 3, 5)] + [(3, 2, m) for m in (0, 2, 4)]
X_DOWN = [(0, 1, m) for m in (1, 3, 5, 0, 2, 4)] + [(1, 2, m) for m in (1, 3, 5)]
ROUNDS = 4


def at_slot(slot):
    return SLOTS.index(slot)


def kernel(
    a_hbm, f_hbm, diag_ref, weight_ref, pattern_ref, ids_ref,
    out_hbm, density_ref,
    a_all, f_all, acc, coarse, wide, out_vmem, part, red, pol,
    load_sem, out_sem, f_send, f_recv, a_send, a_recv, red_send, red_recv, pol_send, pol_recv, token,
):
    pole, row, col = lax.axis_index("pole"), lax.axis_index("row"), lax.axis_index("col")
    n_pole = lax.axis_size("pole")
    y, z = row // 2, row % 2
    rows, depth = a_all.shape[1], a_all.shape[2]
    unit, sixth, third = f_all.shape[1] // UNITS, rows // 6, rows // 3
    blocks = coarse.shape[0] // 4
    rblk = depth // blocks

    def row_of(slot):
        return ((y + slot[0]) % 4) * 2 + (z + slot[1]) % 2

    x_up, x_down = {"col": (col + 1) % 4}, {"col": (col + 3) % 4}
    y_up, y_down, z_swap = {"row": row_of(YN)}, {"row": row_of(YP)}, {"row": row_of(ZP)}
    z_far = {"pole": (pole + n_pole - 2 + 4 * z) % n_pole, "row": row_of(ZP)}
    core = {"pole": pole + 1 - 2 * (pole % 2)}

    def signal(sem, devices):
        for device in devices:
            pl.semaphore_signal(sem, inc=1, device_id=device, device_id_type=MESH)

    own_rows = pltpu.make_async_copy(a_hbm.at[0], a_all.at[0], load_sem.at[4])
    loads = []
    for q in range(4):
        source = pl.ds(pl.multiple_of(((col + q) % 4) * depth, depth), depth)
        loads.append(
            pltpu.make_async_copy(f_hbm.at[0, source], f_all.at[0, pl.ds(q * depth, depth)], load_sem.at[q])
        )
    for q in (0, 2, 1, 3):
        loads[q].start()

    barrier = pltpu.get_barrier_semaphore()
    friends = [x_up, x_down, y_up, y_down, z_swap, z_far, core]
    signal(barrier, friends)
    own_rows.start()

    def f_copies(link, plan, device):
        copies = []
        for i, (here, there, first, count) in enumerate(plan):
            span = pl.ds(first * unit, count * unit)
            copies.append(
                pltpu.make_async_remote_copy(
                    src_ref=f_all.at[at_slot(here), span],
                    dst_ref=f_all.at[at_slot(there), span],
                    send_sem=f_send.at[link, i],
                    recv_sem=f_recv.at[link, i],
                    device_id=device,
                    device_id_type=MESH,
                )
            )
        return copies

    def a_copies(link, plan, device):
        copies = []
        for i, (here, there, m) in enumerate(plan):
            span = pl.ds(m * sixth, sixth)
            copies.append(
                pltpu.make_async_remote_copy(
                    src_ref=a_hbm.at[0, span] if here == 0 else a_all.at[here, span],
                    dst_ref=a_all.at[there, span],
                    send_sem=a_send.at[link, i],
                    recv_sem=a_recv.at[link, i],
                    device_id=device,
                    device_id_type=MESH,
                )
            )
        return copies

    yu, yd, zs = f_copies(0, Y_UP, y_up), f_copies(1, Y_DOWN, y_down), f_copies(2, Z_SWAP, z_swap)
    xu, xd = a_copies(0, X_UP, x_up), a_copies(1, X_DOWN, x_down)

    def start(copies, *which):
        for i in which:
            copies[i].start()

    def arrived(copies, *which):
        for i in which:
            copies[i].wait_recv()

    ids = ids_ref[pl.ds(row * 4 + col, 1), :]
    onehot = jnp.where(ids == lax.broadcasted_iota(jnp.int32, (pattern_ref.shape[0], ids.shape[1]), 0), 1.0, 0.0)
    coarse[...] = lax.dot_general(
        pattern_ref[...].astype(F32).astype(BF16), onehot.astype(BF16), (((0,), (0,)), ((), ())),
        preferred_element_type=F32,
    )

    def mask_quarter(q):
        loads[q].wait()
        first = ((col + q) % 4) * blocks

        def body(j, carry):
            span = pl.ds(pl.multiple_of(q * depth + j * rblk, rblk), rblk)
            mask = coarse[pl.ds(first + j, 1), :].astype(BF16)
            f_all[0, span, :] = f_all[0, span, :] * mask
            return carry

        lax.fori_loop(0, blocks, body, 0)

    mask_quarter(0)
    pl.semaphore_wait(barrier, len(friends))
    start(xu, 0)
    start(xd, 0)
    start(yu, 0)
    start(zs, 0)
    mask_quarter(2)
    start(yd, 0)
    start(xu, 1)
    start(xd, 1)
    mask_quarter(1)
    start(yu, 1)
    start(zs, 1)
    mask_quarter(3)
    start(yd, 1)
    start(xu, 2)
    start(xd, 2)
    start(yu, 2)
    start(yd, 2)
    start(zs, 2, 3)
    start(xu, 3, 4, 5)
    start(xd, 3, 4, 5)

    def tokens(which):
        signal(token.at[which], [z_swap, z_far, core])
        pl.semaphore_wait(token.at[which], 3)

    begun = set()

    def multiply(slots, first, count, chunks=(0, 1, 2)):
        q = first * unit // depth
        where = slice(chunks[0] * third, (chunks[-1] + 1) * third)
        span = slice(first * unit, (first + count) * unit)
        right = [f_all[at_slot(s), span, :] for s in slots]
        right = right[0] if len(right) == 1 else jnp.concatenate(right, axis=1)
        left = a_all[q, where, first * unit - q * depth : (first + count) * unit - q * depth]
        product = jnp.dot(left, right, preferred_element_type=F32)
        width = product.shape[1] // len(slots)
        for i, slot in enumerate(slots):
            for j, c in enumerate(chunks):
                s, here = at_slot(slot), slice(c * third, (c + 1) * third)
                term = product[j * third : (j + 1) * third, i * width : (i + 1) * width]
                acc[s, here, :] = acc[s, here, :] + term if (slot, c) in begun else term
                begun.add((slot, c))

    own_span = pl.ds(pl.multiple_of(((row * rows // depth - col + 4) % 4) * depth + (row * rows) % depth, rows), rows)
    reds = []

    def reduce_rows(slot):
        s = at_slot(slot)
        terms = f_all[s, own_span, :].astype(F32) * acc[s]
        sums = jnp.sum(terms.reshape(rows // 8, 8, terms.shape[1]), axis=0)
        if slot == OWN:
            red[0] = sums
            return
        part[s] = sums
        back = at_slot(((-slot[0]) % 4, slot[1]))
        copy = pltpu.make_async_remote_copy(
            src_ref=part.at[s],
            dst_ref=red.at[back],
            send_sem=red_send.at[s],
            recv_sem=red_recv.at[back],
            device_id={"row": row_of(slot)},
            device_id_type=MESH,
        )
        copy.start()
        reds.append(copy)

    def place(slot):
        wide[pl.ds(row_of(slot), rows, stride=8), :] = acc[at_slot(slot)]

    own_rows.wait()
    arrived(zs, 0)
    multiply([OWN, ZP], 0, 6)
    arrived(yu, 0, 1)
    start(yu, 3, 4)
    arrived(yd, 0, 1)
    start(yd, 3, 4)
    tokens(0)
    arrived(xu, 0, 1, 2)
    start(xu, 6, 7, 8)
    arrived(xd, 0, 1, 2)
    start(xd, 6, 7, 8)
    tokens(1)
    arrived(zs, 1, 2, 3)
    start(yu, 5, 6, 7)
    start(yd, 5, 6, 7)
    arrived(yu, 2)
    arrived(yd, 2)
    start(zs, 4, 5)
    multiply([YN, YP], 0, 6)
    tokens(2)
    arrived(yu, 3, 4)
    arrived(yd, 3, 4)
    start(zs, 6, 7, 8, 9)
    arrived(xu, 3, 4, 5)
    arrived(xd, 3, 4, 5)
    multiply([OWN, ZP], 6, 6)
    multiply([OWN, ZP], 18, 4)
    multiply([OWN], 22, 2)
    arrived(yu, 5)
    start(yu, 8, 9, 10)
    arrived(yd, 5)
    start(yd, 8, 9, 10)
    tokens(3)
    multiply([YN, YP], 6, 4)
    multiply([YP], 10, 2)
    multiply([YN, YP], 18, 6)
    arrived(xu, 6)
    arrived(xd, 6)
    multiply([OWN, ZP], 12, 6, (0,))
    multiply([YN, YP], 14, 4, (0,))
    multiply([YN], 12, 2, (0,))
    arrived(zs, 4, 5)
    multiply([YNZ, YPZ], 18, 6)
    arrived(yu, 6, 7)
    arrived(yd, 6, 7)
    multiply([YNZ, YPZ], 0, 6)
    multiply([YNZ, YPZ], 6, 6)
    arrived(xu, 7)
    arrived(xd, 7)
    multiply([OWN, ZP], 12, 6, (1,))
    multiply([YN, YP], 14, 4, (1,))
    multiply([YN], 12, 2, (1,))
    multiply([YNZ, YPZ], 12, 6, (0, 1))
    arrived(zs, 6)
    multiply([YF, YFZ], 12, 6, (0, 1))
    arrived(yu, 8)
    multiply([YF, YFZ], 0, 3)
    arrived(yd, 8)
    multiply([YF, YFZ], 6, 3)
    arrived(zs, 7)
    multiply([YF, YFZ], 18, 3)
    arrived(xu, 8)
    arrived(xd, 8)
    multiply([YF, YFZ], 12, 6, (2,))
    multiply([YNZ, YPZ], 12, 6, (2,))
    reduce_rows(YNZ)
    reduce_rows(YPZ)
    arrived(yu, 9)
    multiply([YF, YFZ], 3, 3)
    arrived(yd, 9)
    multiply([YF, YFZ], 9, 3)
    arrived(zs, 8)
    multiply([YF, YFZ], 21, 3)
    reduce_rows(YFZ)
    reduce_rows(YF)
    multiply([OWN, ZP], 12, 6, (2,))
    multiply([YN, YP], 14, 4, (2,))
    multiply([YN], 12, 2, (2,))
    arrived(yu, 10)
    multiply([YP], 12, 2)
    reduce_rows(YP)
    arrived(yd, 10)
    multiply([YN], 10, 2)
    reduce_rows(YN)
    arrived(zs, 9)
    multiply([ZP], 22, 2)
    reduce_rows(ZP)
    reduce_rows(OWN)
    for slot in SLOTS:
        place(slot)

    for copy in reds:
        copy.wait_recv()
    total = red[0]
    for s in range(1, 8):
        total = total + red[s]
    inner = jnp.sum(total, axis=0, keepdims=True)
    weighted = weight_ref[0] * (diag_ref[...] + inner)
    pol[pole] = jnp.broadcast_to(weighted, pol.shape[1:])
    pols = []
    for d in range(1, n_pole):
        copy = pltpu.make_async_remote_copy(
            src_ref=pol.at[pole],
            dst_ref=pol.at[pole],
            send_sem=pol_send.at[d],
            recv_sem=pol_recv.at[d],
            device_id={"pole": (pole + d) % n_pole},
            device_id_type=MESH,
        )
        copy.start()
        pols.append(copy)

    outs = []
    for c in range(3):
        def body(j, carry, c=c):
            base = c * third + j * 32
            block = wide[pl.ds(pl.multiple_of(base * 8, 256), 256), :]
            out_vmem[pl.ds(pl.multiple_of(base, 32), 32)] = (-block).reshape(32, 8, block.shape[1]).astype(BF16)
            return carry

        lax.fori_loop(0, third // 32, body, 0)
        span = pl.ds(c * third, third)
        outs.append(pltpu.make_async_copy(out_vmem.at[span], out_hbm.at[span], out_sem.at[c]))
        outs[-1].start()

    for copy in pols:
        copy.wait_recv()
    density = pol[0]
    for p in range(1, n_pole):
        density = density + pol[p]
    density_ref[...] = density[:1]

    for copies in (yu, yd, zs, xu, xd, reds, pols):
        for copy in copies:
            copy.wait_send()
    for copy in outs:
        copy.wait()


def per_device(ancestor_inverse, factor_cols, diag_inverse, pole_weights, block_pattern, supernode_ids):
    _, rows, depth = ancestor_inverse.shape
    _, height, width = factor_cols.shape
    blocks = block_pattern.shape[0]
    vmem = pl.BlockSpec(memory_space=pltpu.VMEM)
    anywhere = pl.BlockSpec(memory_space=pl.ANY)
    dma = pltpu.SemaphoreType.DMA
    links = max(len(Y_UP), len(Z_SWAP))
    out, density = pl.pallas_call(
        kernel,
        out_shape=(
            jax.ShapeDtypeStruct((rows, 8, width), BF16),
            jax.ShapeDtypeStruct((1, width), F32),
        ),
        in_specs=[anywhere, anywhere, vmem, pl.BlockSpec(memory_space=pltpu.SMEM), vmem, vmem],
        out_specs=(anywhere, vmem),
        scratch_shapes=[
            pltpu.VMEM((4, rows, depth), BF16),
            pltpu.VMEM((8, height, width), BF16),
            pltpu.VMEM((8, rows, width), F32),
            pltpu.VMEM((blocks, width), F32),
            pltpu.VMEM((rows * 8, width), F32),
            pltpu.VMEM((rows, 8, width), BF16),
            pltpu.VMEM((8, 8, width), F32),
            pltpu.VMEM((8, 8, width), F32),
            pltpu.VMEM((8, 8, width), F32),
            dma((5,)),
            dma((8,)),
            dma((3, links)),
            dma((3, links)),
            dma((2, len(X_UP))),
            dma((2, len(X_UP))),
            dma((8,)),
            dma((8,)),
            dma((8,)),
            dma((8,)),
            pltpu.SemaphoreType.REGULAR((ROUNDS,)),
        ],
        compiler_params=pltpu.CompilerParams(
            collective_id=0, has_side_effects=True, vmem_limit_bytes=56 * 1024 * 1024
        ),
        cost_estimate=pl.CostEstimate(
            flops=2 * rows * height * 8 * width, bytes_accessed=6 * 1024 * 1024, transcendentals=0
        ),
    )(
        ancestor_inverse,
        factor_cols,
        diag_inverse,
        pole_weights,
        block_pattern.T,
        supernode_ids.reshape(-1, width),
    )
    return out.reshape(1, rows, 8, 1, width), density.reshape(width)


def solution(mesh):
    in_specs = (
        P("pole", "row", "col"),
        P("pole", None, ("row", "col")),
        P("pole", ("row", "col")),
        P("pole"),
        P(),
        P(),
    )
    out_specs = (P("pole", "row", None, "col", None), P(("row", "col")))
    return jax.shard_map(per_device, mesh=mesh, in_specs=in_specs, out_specs=out_specs, check_vma=False)
```

time: 114 us -> 108 us (0.947)
  Pallas kernels: 109 us -> 103 us
    pallas_call x1, Pallas kernels: 109 us -> 103 us  [per_device(): pl.pallas_call(kernel, out_shape=(jax.ShapeDtypeStruct((rows, 8, width),...]
where the time goes in v2:
time: 108 us
  Pallas kernels  103 us (95%)
  local copies, waits for them, and re-layouts  3.17 us (3%)
  between operations  1.29 us (1%)
    pallas_call x1, Pallas kernels, per_device(): pl.pallas_call(kernel, out_shape=(jax.ShapeDtypeStruct((rows, 8, width),...  103 us
    unnamed x4, local copies, waits for them, and re-layouts  3.17 us

profile of v2, /device:TPU:1, one launch (start us, length us, event | category | flops | bytes accessed | tf_op | source)
XLA Modules:
  0.0 107.9 jit_solution(6567566036133950871)
XLA Ops:
  1.3 103.4 %shard_map.77 = (bf16[768,8,128]{2,1,0:T(8,128)(2,1)}, f32[1,128]{1,0:T(1,128)}) custom-call(bf16[1,768,1536]{2,1,0:T(8,128)(2,1)} %a_hbm.1, bf16[1,6144,128]{2,1,0:T(8,128)(2,1)} %f_hbm.1, f32[1,128]{1,0:T(1,128)} %diag_ref.1, f32[1]{0:T(128)S(6)} %copy.11.weight_ref, s32[32,48]{1,0:T(8,128)} %bitcast.7, s32[32,128]{1,0:T(8,128)} %bitcast.8), custom_call_target="tpu_custom_call" | custom-call | flops 9663676416 | bytes 6291456 | tf_op jit(solution)/shard_map/pallas_call | solution.py:369
  104.7 0.0 copy-start
  104.7 2.7 %copy.12 = bf16[1,768,8,1,128]{4,2,3,1,0:T(8,128)(2,1)} copy(bf16[1,768,8,1,128]{4,2,3,1,0:T(8,128)(2,1)} %bitcast.6) | data formatting | bytes 3145728
  107.4 0.0 copy-done
  107.4 0.5 copy.13
Async XLA Ops:
  104.7 2.7 %copy-start = (f32[1,128]{1,0:T(1,128)S(1)}, f32[1,128]{1,0:T(1,128)}, u32[]{:S(2)}) copy-start(f32[1,128]{1,0:T(1,128)} %get-tuple-element.5) | copy-start | bytes 1540

commit v3 on v2

--- a/solution.py
+++ b/solution.py
@@ -16,24 +16,24 @@
 SLOTS = [OWN, ZP, YN, YP, YNZ, YPZ, YF, YFZ]
 
 Y_UP = [
-    (OWN, YP, 0, 6), (OWN, YP, 6, 6), (OWN, YP, 14, 10),
+    (OWN, YP, 0, 6), (OWN, YP, 6, 6), (OWN, YP, 16, 8),
     (YP, YF, 0, 6), (YP, YF, 6, 6),
-    (ZP, YPZ, 0, 6), (ZP, YPZ, 6, 6), (ZP, YPZ, 12, 2),
-    (YPZ, YFZ, 0, 3), (YPZ, YFZ, 3, 3),
-    (OWN, YP, 12, 2),
+    (ZP, YPZ, 0, 6), (ZP, YPZ, 6, 4), (ZP, YPZ, 12, 4),
+    (YPZ, YFZ, 0, 6),
+    (OWN, YP, 12, 2), (OWN, YP, 14, 2),
 ]
 Y_DOWN = [
-    (OWN, YN, 12, 6), (OWN, YN, 18, 6), (OWN, YN, 0, 10),
+    (OWN, YN, 12, 6), (OWN, YN, 18, 6), (OWN, YN, 0, 8),
     (YN, YF, 12, 6), (YN, YF, 18, 6),
     (ZP, YNZ, 6, 6), (ZP, YNZ, 0, 6), (ZP, YNZ, 12, 2),
-    (YNZ, YFZ, 6, 3), (YNZ, YFZ, 9, 3),
-    (OWN, YN, 10, 2),
+    (YNZ, YFZ, 6, 6),
+    (OWN, YN, 8, 2), (OWN, YN, 10, 2),
 ]
 Z_SWAP = [
-    (OWN, ZP, 0, 6), (OWN, ZP, 6, 6), (OWN, ZP, 12, 6), (OWN, ZP, 18, 4),
-    (YN, YNZ, 14, 10), (YP, YPZ, 14, 10),
-    (YF, YFZ, 12, 6), (YF, YFZ, 18, 3), (YF, YFZ, 21, 3),
-    (OWN, ZP, 22, 2),
+    (OWN, ZP, 0, 6), (OWN, ZP, 6, 6), (OWN, ZP, 12, 6), (OWN, ZP, 18, 2),
+    (YN, YNZ, 14, 10), (YP, YPZ, 16, 8), (YP, YPZ, 10, 2),
+    (YF, YFZ, 12, 6), (YF, YFZ, 18, 6),
+    (OWN, ZP, 20, 2), (OWN, ZP, 22, 2),
 ]
 X_UP = [(0, 3, m) for m in (0, 2, 4, 1, 3, 5)] + [(3, 2, m) for m in (0, 2, 4)]
 X_DOWN = [(0, 1, m) for m in (1, 3, 5, 0, 2, 4)] + [(1, 2, m) for m in (1, 3, 5)]
@@ -45,10 +45,10 @@
 
 
 def kernel(
-    a_hbm, f_hbm, diag_ref, weight_ref, pattern_ref, ids_ref,
-    out_hbm, density_ref,
-    a_all, f_all, acc, coarse, wide, out_vmem, part, red, pol,
-    load_sem, out_sem, f_send, f_recv, a_send, a_recv, red_send, red_recv, pol_send, pol_recv, token,
+    a_hbm, f_hbm, diag_hbm, weight_ref, pattern_hbm, ids_hbm,
+    out_ref, density_ref,
+    a_all, f_all, acc, coarse, wide, diag_ref, pattern_ref, ids_ref, part, red, pol,
+    load_sem, f_send, f_recv, a_send, a_recv, red_send, red_recv, pol_send, pol_recv, token,
 ):
     pole, row, col = lax.axis_index("pole"), lax.axis_index("row"), lax.axis_index("col")
     n_pole = lax.axis_size("pole")
@@ -77,12 +77,18 @@
         loads.append(
             pltpu.make_async_copy(f_hbm.at[0, source], f_all.at[0, pl.ds(q * depth, depth)], load_sem.at[q])
         )
-    for q in (0, 2, 1, 3):
-        loads[q].start()
+    small = [
+        pltpu.make_async_copy(source, target, load_sem.at[5 + i])
+        for i, (source, target) in enumerate([(ids_hbm, ids_ref), (pattern_hbm, pattern_ref), (diag_hbm, diag_ref)])
+    ]
 
     barrier = pltpu.get_barrier_semaphore()
     friends = [x_up, x_down, y_up, y_down, z_swap, z_far, core]
     signal(barrier, friends)
+    for copy in small:
+        copy.start()
+    for q in (0, 2, 1, 3):
+        loads[q].start()
     own_rows.start()
 
     def f_copies(link, plan, device):
@@ -128,6 +134,8 @@
         for i in which:
             copies[i].wait_recv()
 
+    for copy in small:
+        copy.wait()
     ids = ids_ref[pl.ds(row * 4 + col, 1), :]
     onehot = jnp.where(ids == lax.broadcasted_iota(jnp.int32, (pattern_ref.shape[0], ids.shape[1]), 0), 1.0, 0.0)
     coarse[...] = lax.dot_general(
@@ -225,6 +233,7 @@
     start(yu, 3, 4)
     arrived(yd, 0, 1)
     start(yd, 3, 4)
+    start(zs, 4)
     tokens(0)
     arrived(xu, 0, 1, 2)
     start(xu, 6, 7, 8)
@@ -235,80 +244,82 @@
     start(yu, 5, 6, 7)
     start(yd, 5, 6, 7)
     arrived(yu, 2)
+    start(zs, 5, 6)
     arrived(yd, 2)
-    start(zs, 4, 5)
     multiply([YN, YP], 0, 6)
     tokens(2)
     arrived(yu, 3, 4)
     arrived(yd, 3, 4)
-    start(zs, 6, 7, 8, 9)
+    start(zs, 7, 8, 9, 10)
     arrived(xu, 3, 4, 5)
     arrived(xd, 3, 4, 5)
     multiply([OWN, ZP], 6, 6)
-    multiply([OWN, ZP], 18, 4)
-    multiply([OWN], 22, 2)
+    multiply([OWN, ZP], 18, 2)
+    multiply([OWN], 20, 4)
     arrived(yu, 5)
     start(yu, 8, 9, 10)
     arrived(yd, 5)
     start(yd, 8, 9, 10)
     tokens(3)
-    multiply([YN, YP], 6, 4)
-    multiply([YP], 10, 2)
+    multiply([YN, YP], 6, 2)
+    multiply([YP], 8, 4)
     multiply([YN, YP], 18, 6)
+    arrived(zs, 4, 5, 6)
+    multiply([YNZ, YPZ], 18, 6)
     arrived(xu, 6)
     arrived(xd, 6)
     multiply([OWN, ZP], 12, 6, (0,))
-    multiply([YN, YP], 14, 4, (0,))
-    multiply([YN], 12, 2, (0,))
-    arrived(zs, 4, 5)
-    multiply([YNZ, YPZ], 18, 6)
-    arrived(yu, 6, 7)
-    arrived(yd, 6, 7)
+    multiply([YN, YP], 16, 2, (0,))
+    multiply([YN], 12, 4, (0,))
+    arrived(yu, 6)
+    multiply([YNZ, YPZ], 6, 6)
+    arrived(yd, 6)
     multiply([YNZ, YPZ], 0, 6)
-    multiply([YNZ, YPZ], 6, 6)
+    arrived(yu, 7)
+    arrived(yd, 7)
+    multiply([YNZ, YPZ], 12, 6, (0,))
+    arrived(zs, 7)
+    multiply([YF, YFZ], 12, 6, (0,))
     arrived(xu, 7)
     arrived(xd, 7)
     multiply([OWN, ZP], 12, 6, (1,))
-    multiply([YN, YP], 14, 4, (1,))
-    multiply([YN], 12, 2, (1,))
-    multiply([YNZ, YPZ], 12, 6, (0, 1))
-    arrived(zs, 6)
-    multiply([YF, YFZ], 12, 6, (0, 1))
+    multiply([YN, YP], 16, 2, (1,))
+    multiply([YN], 12, 4, (1,))
+    multiply([YNZ, YPZ], 12, 6, (1,))
+    multiply([YF, YFZ], 12, 6, (1,))
     arrived(yu, 8)
-    multiply([YF, YFZ], 0, 3)
+    multiply([YF, YFZ], 0, 6)
     arrived(yd, 8)
-    multiply([YF, YFZ], 6, 3)
-    arrived(zs, 7)
-    multiply([YF, YFZ], 18, 3)
+    multiply([YF, YFZ], 6, 6)
+    arrived(zs, 8)
+    multiply([YF, YFZ], 18, 6)
     arrived(xu, 8)
     arrived(xd, 8)
     multiply([YF, YFZ], 12, 6, (2,))
+    reduce_rows(YFZ)
+    reduce_rows(YF)
     multiply([YNZ, YPZ], 12, 6, (2,))
     reduce_rows(YNZ)
     reduce_rows(YPZ)
+    multiply([OWN, ZP], 12, 6, (2,))
+    multiply([YN, YP], 16, 2, (2,))
+    multiply([YN], 12, 4, (2,))
     arrived(yu, 9)
-    multiply([YF, YFZ], 3, 3)
+    multiply([YP], 12, 2)
     arrived(yd, 9)
-    multiply([YF, YFZ], 9, 3)
-    arrived(zs, 8)
-    multiply([YF, YFZ], 21, 3)
-    reduce_rows(YFZ)
-    reduce_rows(YF)
-    multiply([OWN, ZP], 12, 6, (2,))
-    multiply([YN, YP], 14, 4, (2,))
-    multiply([YN], 12, 2, (2,))
+    multiply([YN], 8, 2)
+    arrived(zs, 9)
+    multiply([ZP], 20, 2)
+    reduce_rows(OWN)
     arrived(yu, 10)
-    multiply([YP], 12, 2)
+    multiply([YP], 14, 2)
     reduce_rows(YP)
     arrived(yd, 10)
     multiply([YN], 10, 2)
     reduce_rows(YN)
-    arrived(zs, 9)
+    arrived(zs, 10)
     multiply([ZP], 22, 2)
     reduce_rows(ZP)
-    reduce_rows(OWN)
-    for slot in SLOTS:
-        place(slot)
 
     for copy in reds:
         copy.wait_recv()
@@ -319,7 +330,7 @@
     weighted = weight_ref[0] * (diag_ref[...] + inner)
     pol[pole] = jnp.broadcast_to(weighted, pol.shape[1:])
     pols = []
-    for d in range(1, n_pole):
+    for d in sorted(range(1, n_pole), key=lambda d: abs(d - n_pole // 2)):
         copy = pltpu.make_async_remote_copy(
             src_ref=pol.at[pole],
             dst_ref=pol.at[pole],
@@ -331,18 +342,16 @@
         copy.start()
         pols.append(copy)
 
-    outs = []
-    for c in range(3):
-        def body(j, carry, c=c):
-            base = c * third + j * 32
-            block = wide[pl.ds(pl.multiple_of(base * 8, 256), 256), :]
-            out_vmem[pl.ds(pl.multiple_of(base, 32), 32)] = (-block).reshape(32, 8, block.shape[1]).astype(BF16)
-            return carry
-
-        lax.fori_loop(0, third // 32, body, 0)
-        span = pl.ds(c * third, third)
-        outs.append(pltpu.make_async_copy(out_vmem.at[span], out_hbm.at[span], out_sem.at[c]))
-        outs[-1].start()
+    for slot in SLOTS:
+        place(slot)
+
+    def body(j, carry):
+        base = pl.multiple_of(j * 32, 32)
+        block = wide[pl.ds(pl.multiple_of(base * 8, 256), 256), :]
+        out_ref[pl.ds(base, 32)] = (-block).reshape(32, 8, block.shape[1]).astype(BF16)
+        return carry
+
+    lax.fori_loop(0, rows // 32, body, 0)
 
     for copy in pols:
         copy.wait_recv()
@@ -354,8 +363,6 @@
     for copies in (yu, yd, zs, xu, xd, reds, pols):
         for copy in copies:
             copy.wait_send()
-    for copy in outs:
-        copy.wait()
 
 
 def per_device(ancestor_inverse, factor_cols, diag_inverse, pole_weights, block_pattern, supernode_ids):
@@ -369,22 +376,23 @@
     out, density = pl.pallas_call(
         kernel,
         out_shape=(
-            jax.ShapeDtypeStruct((rows, 8, width), BF16),
-            jax.ShapeDtypeStruct((1, width), F32),
+            pltpu.VMEM((rows, 8, width), BF16),
+            pltpu.VMEM((1, width), F32),
         ),
-        in_specs=[anywhere, anywhere, vmem, pl.BlockSpec(memory_space=pltpu.SMEM), vmem, vmem],
-        out_specs=(anywhere, vmem),
+        in_specs=[anywhere, anywhere, anywhere, pl.BlockSpec(memory_space=pltpu.SMEM), anywhere, anywhere],
+        out_specs=(vmem, vmem),
         scratch_shapes=[
             pltpu.VMEM((4, rows, depth), BF16),
             pltpu.VMEM((8, height, width), BF16),
             pltpu.VMEM((8, rows, width), F32),
             pltpu.VMEM((blocks, width), F32),
             pltpu.VMEM((rows * 8, width), F32),
-            pltpu.VMEM((rows, 8, width), BF16),
+            pltpu.VMEM((1, width), F32),
+            pltpu.VMEM(block_pattern.shape[::-1], jnp.int32),
+            pltpu.VMEM((supernode_ids.size // width, width), jnp.int32),
             pltpu.VMEM((8, 8, width), F32),
             pltpu.VMEM((8, 8, width), F32),
             pltpu.VMEM((8, 8, width), F32),
-            dma((5,)),
             dma((8,)),
             dma((3, links)),
             dma((3, links)),
@@ -397,7 +405,7 @@
             pltpu.SemaphoreType.REGULAR((ROUNDS,)),
         ],
         compiler_params=pltpu.CompilerParams(
-            collective_id=0, has_side_effects=True, vmem_limit_bytes=56 * 1024 * 1024
+            collective_id=0, has_side_effects=True, vmem_limit_bytes=63_400_000
         ),
         cost_estimate=pl.CostEstimate(
             flops=2 * rows * height * 8 * width, bytes_accessed=6 * 1024 * 1024, transcendentals=0

time: 108 us -> 107 us (level)
  local copies, waits for them, and re-layouts: 3.17 us -> 1.66 us
    unnamed x4 -> x2, local copies, waits for them, and re-layouts: 3.17 us -> 1.66 us
where the time goes in v3:
time: 107 us
  Pallas kernels  104 us (97%)
  local copies, waits for them, and re-layouts  1.66 us (2%)
  between operations  1.29 us (1%)
    pallas_call x1, Pallas kernels, per_device(): pl.pallas_call(kernel, out_shape=(pltpu.VMEM((rows, 8, width), BF16), plt...  104 us

profile of v3, /device:TPU:1, one launch (start us, length us, event | category | flops | bytes accessed | tf_op | source)
XLA Modules:
  0.0 106.6 jit_solution(3801985901209590423)
XLA Ops:
  1.3 103.7 %shard_map.77 = (bf16[768,8,128]{2,1,0:T(8,128)(2,1)S(1)}, f32[1,128]{1,0:T(1,128)S(1)}) custom-call(bf16[1,768,1536]{2,1,0:T(8,128)(2,1)} %a_hbm.1, bf16[1,6144,128]{2,1,0:T(8,128)(2,1)} %f_hbm.1, f32[1,128]{1,0:T(1,128)} %diag_hbm.1, f32[1]{0:T(128)S(6)} %copy.13.weight_ref, s32[32,48]{1,0:T(8,128)} %bitcast.8, s32[32,128]{1,0:T(8,128)} %bitcast.9), custom_call_target="tpu_custom_call" | custom-call | flops 9663676416 | bytes 6291456 | tf_op jit(solution)/shard_map/pallas_call | solution.py:376
  105.0 1.1 %copy.11 = bf16[1,768,8,1,128]{4,2,3,1,0:T(8,128)(2,1)} copy(bf16[1,768,8,1,128]{4,2,3,1,0:T(8,128)(2,1)S(1)} %bitcast.6) | data formatting | bytes 3145728
  106.1 0.5 copy.12

commit v4 on v3

--- a/solution.py
+++ b/solution.py
@@ -16,27 +16,29 @@
 SLOTS = [OWN, ZP, YN, YP, YNZ, YPZ, YF, YFZ]
 
 Y_UP = [
-    (OWN, YP, 0, 6), (OWN, YP, 6, 6), (OWN, YP, 16, 8),
-    (YP, YF, 0, 6), (YP, YF, 6, 6),
-    (ZP, YPZ, 0, 6), (ZP, YPZ, 6, 4), (ZP, YPZ, 12, 4),
+    (OWN, YP, 0, 6), (OWN, YP, 18, 6), (OWN, YP, 12, 6), (OWN, YP, 6, 2),
+    (YP, YF, 0, 6), (YP, YF, 18, 6),
+    (ZP, YPZ, 0, 6), (ZP, YPZ, 6, 6), (ZP, YPZ, 12, 2),
     (YPZ, YFZ, 0, 6),
-    (OWN, YP, 12, 2), (OWN, YP, 14, 2),
+    (OWN, YP, 8, 3), (OWN, YP, 11, 1),
 ]
 Y_DOWN = [
-    (OWN, YN, 12, 6), (OWN, YN, 18, 6), (OWN, YN, 0, 8),
-    (YN, YF, 12, 6), (YN, YF, 18, 6),
+    (OWN, YN, 12, 6), (OWN, YN, 18, 6), (OWN, YN, 6, 6), (OWN, YN, 0, 2),
+    (YN, YF, 12, 6), (YN, YF, 6, 6),
     (ZP, YNZ, 6, 6), (ZP, YNZ, 0, 6), (ZP, YNZ, 12, 2),
     (YNZ, YFZ, 6, 6),
-    (OWN, YN, 8, 2), (OWN, YN, 10, 2),
+    (OWN, YN, 2, 3), (OWN, YN, 5, 1),
 ]
 Z_SWAP = [
-    (OWN, ZP, 0, 6), (OWN, ZP, 6, 6), (OWN, ZP, 12, 6), (OWN, ZP, 18, 2),
-    (YN, YNZ, 14, 10), (YP, YPZ, 16, 8), (YP, YPZ, 10, 2),
+    (OWN, ZP, 0, 6), (OWN, ZP, 6, 6), (OWN, ZP, 12, 8),
+    (YN, YNZ, 14, 10), (YP, YPZ, 14, 10),
     (YF, YFZ, 12, 6), (YF, YFZ, 18, 6),
-    (OWN, ZP, 20, 2), (OWN, ZP, 22, 2),
+    (OWN, ZP, 20, 3), (OWN, ZP, 23, 1),
 ]
-X_UP = [(0, 3, m) for m in (0, 2, 4, 1, 3, 5)] + [(3, 2, m) for m in (0, 2, 4)]
-X_DOWN = [(0, 1, m) for m in (1, 3, 5, 0, 2, 4)] + [(1, 2, m) for m in (1, 3, 5)]
+HALVES = [[(0, 10), (20, 10), (40, 4)], [(10, 10), (30, 10), (44, 4)]]
+X_UP = [(0, 3, *m) for m in HALVES[0] + HALVES[1]] + [(3, 2, *m) for m in HALVES[0]]
+X_DOWN = [(0, 1, *m) for m in HALVES[1] + HALVES[0]] + [(1, 2, *m) for m in HALVES[1]]
+CHUNKS = [(0, 20), (20, 40), (40, 48)]
 ROUNDS = 4
 
 
@@ -54,7 +56,7 @@
     n_pole = lax.axis_size("pole")
     y, z = row // 2, row % 2
     rows, depth = a_all.shape[1], a_all.shape[2]
-    unit, sixth, third = f_all.shape[1] // UNITS, rows // 6, rows // 3
+    unit, part_rows = f_all.shape[1] // UNITS, rows // 48
     blocks = coarse.shape[0] // 4
     rblk = depth // blocks
 
@@ -109,8 +111,8 @@
 
     def a_copies(link, plan, device):
         copies = []
-        for i, (here, there, m) in enumerate(plan):
-            span = pl.ds(m * sixth, sixth)
+        for i, (here, there, first, count) in enumerate(plan):
+            span = pl.ds(first * part_rows, count * part_rows)
             copies.append(
                 pltpu.make_async_remote_copy(
                     src_ref=a_hbm.at[0, span] if here == 0 else a_all.at[here, span],
@@ -157,26 +159,26 @@
 
     mask_quarter(0)
     pl.semaphore_wait(barrier, len(friends))
+    start(yu, 0)
+    start(zs, 0)
     start(xu, 0)
     start(xd, 0)
-    start(yu, 0)
-    start(zs, 0)
     mask_quarter(2)
     start(yd, 0)
+    mask_quarter(1)
+    start(zs, 1)
+    mask_quarter(3)
+    start(yu, 1)
+    start(yd, 1)
+    start(yd, 2)
     start(xu, 1)
     start(xd, 1)
-    mask_quarter(1)
-    start(yu, 1)
-    start(zs, 1)
-    mask_quarter(3)
-    start(yd, 1)
-    start(xu, 2)
-    start(xd, 2)
     start(yu, 2)
-    start(yd, 2)
-    start(zs, 2, 3)
-    start(xu, 3, 4, 5)
-    start(xd, 3, 4, 5)
+    start(zs, 2)
+    start(yu, 3)
+    start(yd, 3)
+    start(xu, 2, 3, 4, 5)
+    start(xd, 2, 3, 4, 5)
 
     def tokens(which):
         signal(token.at[which], [z_swap, z_far, core])
@@ -184,28 +186,41 @@
 
     begun = set()
 
-    def multiply(slots, first, count, chunks=(0, 1, 2)):
+    def product_of(slots, first, count, where):
         q = first * unit // depth
-        where = slice(chunks[0] * third, (chunks[-1] + 1) * third)
         span = slice(first * unit, (first + count) * unit)
         right = [f_all[at_slot(s), span, :] for s in slots]
         right = right[0] if len(right) == 1 else jnp.concatenate(right, axis=1)
         left = a_all[q, where, first * unit - q * depth : (first + count) * unit - q * depth]
-        product = jnp.dot(left, right, preferred_element_type=F32)
+        return jnp.dot(left, right, preferred_element_type=F32)
+
+    def multiply(slots, first, count, chunks=(0, 1, 2)):
+        base = CHUNKS[chunks[0]][0] * part_rows
+        product = product_of(slots, first, count, slice(base, CHUNKS[chunks[-1]][1] * part_rows))
         width = product.shape[1] // len(slots)
         for i, slot in enumerate(slots):
-            for j, c in enumerate(chunks):
-                s, here = at_slot(slot), slice(c * third, (c + 1) * third)
-                term = product[j * third : (j + 1) * third, i * width : (i + 1) * width]
-                acc[s, here, :] = acc[s, here, :] + term if (slot, c) in begun else term
+            for c in chunks:
+                s, begin, end = at_slot(slot), CHUNKS[c][0] * part_rows, CHUNKS[c][1] * part_rows
+                term = product[begin - base : end - base, i * width : (i + 1) * width]
+                acc[s, begin:end, :] = acc[s, begin:end, :] + term if (slot, c) in begun else term
                 begun.add((slot, c))
 
     own_span = pl.ds(pl.multiple_of(((row * rows // depth - col + 4) % 4) * depth + (row * rows) % depth, rows), rows)
     reds = []
 
-    def reduce_rows(slot):
+    def place(slot, total):
+        wide[pl.ds(row_of(slot), rows, stride=8), :] = total
+
+    def finish(pieces):
+        totals = [acc[at_slot(slot)] + product_of([slot], first, count, slice(0, rows)) for slot, first, count in pieces]
+        for (slot, _, _), total in zip(pieces, totals):
+            reduce_rows(slot, total)
+        for (slot, _, _), total in zip(pieces, totals):
+            place(slot, total)
+
+    def reduce_rows(slot, total):
         s = at_slot(slot)
-        terms = f_all[s, own_span, :].astype(F32) * acc[s]
+        terms = f_all[s, own_span, :].astype(F32) * total
         sums = jnp.sum(terms.reshape(rows // 8, 8, terms.shape[1]), axis=0)
         if slot == OWN:
             red[0] = sums
@@ -223,103 +238,85 @@
         copy.start()
         reds.append(copy)
 
-    def place(slot):
-        wide[pl.ds(row_of(slot), rows, stride=8), :] = acc[at_slot(slot)]
-
     own_rows.wait()
     arrived(zs, 0)
     multiply([OWN, ZP], 0, 6)
     arrived(yu, 0, 1)
-    start(yu, 3, 4)
+    start(yu, 4, 5)
     arrived(yd, 0, 1)
-    start(yd, 3, 4)
-    start(zs, 4)
+    start(zs, 3)
+    start(yd, 4)
     tokens(0)
+    arrived(yd, 2)
+    start(yd, 5)
     arrived(xu, 0, 1, 2)
     start(xu, 6, 7, 8)
     arrived(xd, 0, 1, 2)
     start(xd, 6, 7, 8)
+    arrived(zs, 1, 2)
+    start(yu, 6, 7, 8)
+    start(yd, 6, 7, 8)
+    arrived(yu, 2)
+    start(zs, 4)
     tokens(1)
-    arrived(zs, 1, 2, 3)
-    start(yu, 5, 6, 7)
-    start(yd, 5, 6, 7)
-    arrived(yu, 2)
-    start(zs, 5, 6)
-    arrived(yd, 2)
-    multiply([YN, YP], 0, 6)
+    arrived(yu, 3)
+    arrived(yd, 3)
+    multiply([YN, YP], 0, 2)
+    multiply([YP], 2, 4)
     tokens(2)
-    arrived(yu, 3, 4)
-    arrived(yd, 3, 4)
-    start(zs, 7, 8, 9, 10)
+    arrived(yu, 4, 5)
+    arrived(yd, 4, 5)
+    start(zs, 5, 6, 7, 8)
+    tokens(3)
     arrived(xu, 3, 4, 5)
     arrived(xd, 3, 4, 5)
     multiply([OWN, ZP], 6, 6)
     multiply([OWN, ZP], 18, 2)
     multiply([OWN], 20, 4)
-    arrived(yu, 5)
-    start(yu, 8, 9, 10)
-    arrived(yd, 5)
-    start(yd, 8, 9, 10)
-    tokens(3)
+    arrived(yu, 6)
+    start(yu, 9, 10, 11)
+    arrived(yd, 6)
+    start(yd, 9, 10, 11)
     multiply([YN, YP], 6, 2)
-    multiply([YP], 8, 4)
+    multiply([YN], 8, 4)
     multiply([YN, YP], 18, 6)
-    arrived(zs, 4, 5, 6)
+    arrived(zs, 3, 4)
     multiply([YNZ, YPZ], 18, 6)
+    arrived(yu, 7)
+    arrived(yd, 7)
+    multiply([YNZ, YPZ], 0, 6)
+    multiply([YNZ, YPZ], 6, 6)
     arrived(xu, 6)
     arrived(xd, 6)
-    multiply([OWN, ZP], 12, 6, (0,))
-    multiply([YN, YP], 16, 2, (0,))
-    multiply([YN], 12, 4, (0,))
-    arrived(yu, 6)
-    multiply([YNZ, YPZ], 6, 6)
-    arrived(yd, 6)
-    multiply([YNZ, YPZ], 0, 6)
-    arrived(yu, 7)
-    arrived(yd, 7)
-    multiply([YNZ, YPZ], 12, 6, (0,))
-    arrived(zs, 7)
-    multiply([YF, YFZ], 12, 6, (0,))
+    multiply([OWN, ZP, YN, YP], 12, 6, (0,))
+    arrived(yu, 8)
+    arrived(yd, 8)
+    arrived(zs, 5)
+    multiply([YNZ, YPZ, YF, YFZ], 12, 6, (0,))
     arrived(xu, 7)
     arrived(xd, 7)
-    multiply([OWN, ZP], 12, 6, (1,))
-    multiply([YN, YP], 16, 2, (1,))
-    multiply([YN], 12, 4, (1,))
-    multiply([YNZ, YPZ], 12, 6, (1,))
-    multiply([YF, YFZ], 12, 6, (1,))
-    arrived(yu, 8)
+    multiply(SLOTS, 12, 6, (1,))
+    arrived(yu, 9)
     multiply([YF, YFZ], 0, 6)
-    arrived(yd, 8)
+    arrived(yd, 9)
     multiply([YF, YFZ], 6, 6)
-    arrived(zs, 8)
+    arrived(zs, 6)
     multiply([YF, YFZ], 18, 6)
     arrived(xu, 8)
     arrived(xd, 8)
-    multiply([YF, YFZ], 12, 6, (2,))
-    reduce_rows(YFZ)
-    reduce_rows(YF)
-    multiply([YNZ, YPZ], 12, 6, (2,))
-    reduce_rows(YNZ)
-    reduce_rows(YPZ)
-    multiply([OWN, ZP], 12, 6, (2,))
-    multiply([YN, YP], 16, 2, (2,))
-    multiply([YN], 12, 4, (2,))
-    arrived(yu, 9)
-    multiply([YP], 12, 2)
-    arrived(yd, 9)
-    multiply([YN], 8, 2)
-    arrived(zs, 9)
-    multiply([ZP], 20, 2)
-    reduce_rows(OWN)
+    multiply(SLOTS, 12, 6, (2,))
+    for slot in (YFZ, YF, YNZ, YPZ, OWN):
+        reduce_rows(slot, acc[at_slot(slot)])
     arrived(yu, 10)
-    multiply([YP], 14, 2)
-    reduce_rows(YP)
     arrived(yd, 10)
-    multiply([YN], 10, 2)
-    reduce_rows(YN)
-    arrived(zs, 10)
-    multiply([ZP], 22, 2)
-    reduce_rows(ZP)
+    arrived(zs, 7)
+    multiply([YP], 8, 3)
+    multiply([YN], 2, 3)
+    multiply([ZP], 20, 3)
+    arrived(yu, 11)
+    arrived(yd, 11)
+    arrived(zs, 8)
+    finish([(YP, 11, 1), (YN, 5, 1), (ZP, 23, 1)])
 
     for copy in reds:
         copy.wait_recv()
@@ -342,8 +339,8 @@
         copy.start()
         pols.append(copy)
 
-    for slot in SLOTS:
-        place(slot)
+    for slot in (OWN, YNZ, YPZ, YF, YFZ):
+        place(slot, acc[at_slot(slot)])
 
     def body(j, carry):
         base = pl.multiple_of(j * 32, 32)
@@ -363,6 +360,18 @@
     for copies in (yu, yd, zs, xu, xd, reds, pols):
         for copy in copies:
             copy.wait_send()
+
+
+def hand_over(out_ref, density_ref, out_hbm, density_hbm, sems):
+    rows = out_ref.shape[0]
+    copies = [pltpu.make_async_copy(density_ref, density_hbm, sems.at[4])]
+    for i in range(4):
+        span = pl.ds(i * (rows // 4), rows // 4)
+        copies.append(pltpu.make_async_copy(out_ref.at[span], out_hbm.at[span], sems.at[i]))
+    for copy in copies:
+        copy.start()
+    for copy in copies:
+        copy.wait()
 
 
 def per_device(ancestor_inverse, factor_cols, diag_inverse, pole_weights, block_pattern, supernode_ids):
@@ -418,6 +427,17 @@
         block_pattern.T,
         supernode_ids.reshape(-1, width),
     )
+    out, density = pl.pallas_call(
+        hand_over,
+        out_shape=(
+            jax.ShapeDtypeStruct((rows, 8, width), BF16),
+            jax.ShapeDtypeStruct((1, width), F32),
+        ),
+        in_specs=[vmem, vmem],
+        out_specs=(anywhere, anywhere),
+        scratch_shapes=[dma((5,))],
+        compiler_params=pltpu.CompilerParams(vmem_limit_bytes=16 * 1024 * 1024),
+    )(out, density)
     return out.reshape(1, rows, 8, 1, width), density.reshape(width)
 
 

time: 107 us -> 105 us (0.981)
  local copies, waits for them, and re-layouts: 1.66 us -> 0 us
    unnamed x2 -> x0, local copies, waits for them, and re-layouts: 1.66 us -> none
    pallas_call x1, Pallas kernels: 104 us -> 102 us  [per_device(): pl.pallas_call(kernel, out_shape=(pltpu.VMEM((rows, 8, width), BF16), plt...]
    pallas_call x0 -> x1, Pallas kernels: none -> 1.18 us  [per_device(): pl.pallas_call(hand_over, out_shape=(jax.ShapeDtypeStruct((rows, 8, width...]
where the time goes in v4:
time: 105 us
  Pallas kernels  104 us (99%)
  between operations  1.28 us (1%)
    pallas_call x1, Pallas kernels, per_device(): pl.pallas_call(kernel, out_shape=(pltpu.VMEM((rows, 8, width), BF16), plt...  102 us

profile of v4, /device:TPU:1, one launch (start us, length us, event | category | flops | bytes accessed | tf_op | source)
XLA Modules:
  0.0 104.9 jit_solution(13980283237237503695)
XLA Ops:
  1.3 102.5 %shard_map.77 = (bf16[768,8,128]{2,1,0:T(8,128)(2,1)S(1)}, f32[1,128]{1,0:T(1,128)S(1)}) custom-call(bf16[1,768,1536]{2,1,0:T(8,128)(2,1)} %a_hbm.1, bf16[1,6144,128]{2,1,0:T(8,128)(2,1)} %f_hbm.1, f32[1,128]{1,0:T(1,128)} %diag_hbm.1, f32[1]{0:T(128)S(6)} %copy.9.weight_ref, s32[32,48]{1,0:T(8,128)} %bitcast.7, s32[32,128]{1,0:T(8,128)} %bitcast.8), custom_call_target="tpu_custom_call" | custom-call | flops 9663676416 | bytes 6291456 | tf_op jit(solution)/shard_map/pallas_call | solution.py:385
  103.8 1.2 %shard_map.78 = (bf16[768,8,128]{2,1,0:T(8,128)(2,1)}, f32[1,128]{1,0:T(1,128)}) custom-call(bf16[768,8,128]{2,1,0:T(8,128)(2,1)S(1)} %get-tuple-element.6.out_ref, f32[1,128]{1,0:T(1,128)S(1)} %get-tuple-element.7.density_ref), custom_call_target="tpu_custom_call" | custom-call | tf_op jit(solution)/shard_map/pallas_call | solution.py:430

commit v5 on v4

--- a/solution.py
+++ b/solution.py
@@ -14,25 +14,26 @@
 OWN, ZP, YN, YP = (0, 0), (0, 1), (1, 0), (3, 0)
 YNZ, YPZ, YF, YFZ = (1, 1), (3, 1), (2, 0), (2, 1)
 SLOTS = [OWN, ZP, YN, YP, YNZ, YPZ, YF, YFZ]
+NEAR = [YP, YN, ZP]
 
 Y_UP = [
     (OWN, YP, 0, 6), (OWN, YP, 18, 6), (OWN, YP, 12, 6), (OWN, YP, 6, 2),
     (YP, YF, 0, 6), (YP, YF, 18, 6),
     (ZP, YPZ, 0, 6), (ZP, YPZ, 6, 6), (ZP, YPZ, 12, 2),
-    (YPZ, YFZ, 0, 6),
+    (YPZ, YFZ, 0, 3), (YPZ, YFZ, 3, 3),
     (OWN, YP, 8, 3), (OWN, YP, 11, 1),
 ]
 Y_DOWN = [
     (OWN, YN, 12, 6), (OWN, YN, 18, 6), (OWN, YN, 6, 6), (OWN, YN, 0, 2),
     (YN, YF, 12, 6), (YN, YF, 6, 6),
     (ZP, YNZ, 6, 6), (ZP, YNZ, 0, 6), (ZP, YNZ, 12, 2),
-    (YNZ, YFZ, 6, 6),
+    (YNZ, YFZ, 6, 3), (YNZ, YFZ, 9, 3),
     (OWN, YN, 2, 3), (OWN, YN, 5, 1),
 ]
 Z_SWAP = [
     (OWN, ZP, 0, 6), (OWN, ZP, 6, 6), (OWN, ZP, 12, 8),
     (YN, YNZ, 14, 10), (YP, YPZ, 14, 10),
-    (YF, YFZ, 12, 6), (YF, YFZ, 18, 6),
+    (YF, YFZ, 12, 6), (YF, YFZ, 18, 3), (YF, YFZ, 21, 3),
     (OWN, ZP, 20, 3), (OWN, ZP, 23, 1),
 ]
 HALVES = [[(0, 10), (20, 10), (40, 4)], [(10, 10), (30, 10), (44, 4)]]
@@ -49,8 +50,8 @@
 def kernel(
     a_hbm, f_hbm, diag_hbm, weight_ref, pattern_hbm, ids_hbm,
     out_ref, density_ref,
-    a_all, f_all, acc, coarse, wide, diag_ref, pattern_ref, ids_ref, part, red, pol,
-    load_sem, f_send, f_recv, a_send, a_recv, red_send, red_recv, pol_send, pol_recv, token,
+    a_all, f_all, acc, coarse, wide, diag_ref, pattern_ref, ids_ref, part, red, near, late, pol,
+    load_sem, f_send, f_recv, a_send, a_recv, red_send, red_recv, end_send, end_recv, token,
 ):
     pole, row, col = lax.axis_index("pole"), lax.axis_index("row"), lax.axis_index("col")
     n_pole = lax.axis_size("pole")
@@ -207,6 +208,7 @@
 
     own_span = pl.ds(pl.multiple_of(((row * rows // depth - col + 4) % 4) * depth + (row * rows) % depth, rows), rows)
     reds = []
+    far_first = sorted(range(n_pole), key=lambda d: abs(d - n_pole // 2))
 
     def place(slot, total):
         wide[pl.ds(row_of(slot), rows, stride=8), :] = total
@@ -214,14 +216,27 @@
     def finish(pieces):
         totals = [acc[at_slot(slot)] + product_of([slot], first, count, slice(0, rows)) for slot, first, count in pieces]
         for (slot, _, _), total in zip(pieces, totals):
-            reduce_rows(slot, total)
+            k, back = NEAR.index(slot), NEAR.index(((-slot[0]) % 4, slot[1]))
+            near[k] = weight_ref[0] * jnp.sum(row_sums(slot, total), axis=0, keepdims=True)
+            for d in far_first:
+                pltpu.make_async_remote_copy(
+                    src_ref=near.at[k],
+                    dst_ref=late.at[back, pole],
+                    send_sem=end_send.at[0],
+                    recv_sem=end_recv.at[0],
+                    device_id={"pole": (pole + d) % n_pole, "row": row_of(slot)},
+                    device_id_type=MESH,
+                ).start()
         for (slot, _, _), total in zip(pieces, totals):
             place(slot, total)
 
+    def row_sums(slot, total):
+        terms = f_all[at_slot(slot), own_span, :].astype(F32) * total
+        return jnp.sum(terms.reshape(rows // 8, 8, terms.shape[1]), axis=0)
+
     def reduce_rows(slot, total):
         s = at_slot(slot)
-        terms = f_all[s, own_span, :].astype(F32) * total
-        sums = jnp.sum(terms.reshape(rows // 8, 8, terms.shape[1]), axis=0)
+        sums = row_sums(slot, total)
         if slot == OWN:
             red[0] = sums
             return
@@ -266,7 +281,7 @@
     tokens(2)
     arrived(yu, 4, 5)
     arrived(yd, 4, 5)
-    start(zs, 5, 6, 7, 8)
+    start(zs, 5, 6, 7, 8, 9)
     tokens(3)
     arrived(xu, 3, 4, 5)
     arrived(xd, 3, 4, 5)
@@ -274,9 +289,9 @@
     multiply([OWN, ZP], 18, 2)
     multiply([OWN], 20, 4)
     arrived(yu, 6)
-    start(yu, 9, 10, 11)
+    start(yu, 9, 10, 11, 12)
     arrived(yd, 6)
-    start(yd, 9, 10, 11)
+    start(yd, 9, 10, 11, 12)
     multiply([YN, YP], 6, 2)
     multiply([YN], 8, 4)
     multiply([YN, YP], 18, 6)
@@ -288,56 +303,57 @@
     multiply([YNZ, YPZ], 6, 6)
     arrived(xu, 6)
     arrived(xd, 6)
-    multiply([OWN, ZP, YN, YP], 12, 6, (0,))
     arrived(yu, 8)
     arrived(yd, 8)
     arrived(zs, 5)
-    multiply([YNZ, YPZ, YF, YFZ], 12, 6, (0,))
+    multiply(SLOTS, 12, 6, (0,))
+    arrived(yu, 9)
+    arrived(yd, 9)
+    arrived(zs, 6)
+    multiply([YF, YFZ], 0, 3)
+    multiply([YF, YFZ], 6, 3)
+    multiply([YF, YFZ], 18, 3)
     arrived(xu, 7)
     arrived(xd, 7)
     multiply(SLOTS, 12, 6, (1,))
-    arrived(yu, 9)
-    multiply([YF, YFZ], 0, 6)
-    arrived(yd, 9)
-    multiply([YF, YFZ], 6, 6)
-    arrived(zs, 6)
-    multiply([YF, YFZ], 18, 6)
+    arrived(yu, 10)
+    arrived(yd, 10)
+    arrived(zs, 7)
+    multiply([YF, YFZ], 3, 3)
+    multiply([YF, YFZ], 9, 3)
+    multiply([YF, YFZ], 21, 3)
     arrived(xu, 8)
     arrived(xd, 8)
     multiply(SLOTS, 12, 6, (2,))
     for slot in (YFZ, YF, YNZ, YPZ, OWN):
         reduce_rows(slot, acc[at_slot(slot)])
-    arrived(yu, 10)
-    arrived(yd, 10)
-    arrived(zs, 7)
+    arrived(yu, 11)
+    arrived(yd, 11)
+    arrived(zs, 8)
     multiply([YP], 8, 3)
     multiply([YN], 2, 3)
     multiply([ZP], 20, 3)
-    arrived(yu, 11)
-    arrived(yd, 11)
-    arrived(zs, 8)
+    arrived(yu, 12)
+    arrived(yd, 12)
+    arrived(zs, 9)
     finish([(YP, 11, 1), (YN, 5, 1), (ZP, 23, 1)])
 
     for copy in reds:
         copy.wait_recv()
-    total = red[0]
-    for s in range(1, 8):
-        total = total + red[s]
-    inner = jnp.sum(total, axis=0, keepdims=True)
-    weighted = weight_ref[0] * (diag_ref[...] + inner)
-    pol[pole] = jnp.broadcast_to(weighted, pol.shape[1:])
-    pols = []
-    for d in sorted(range(1, n_pole), key=lambda d: abs(d - n_pole // 2)):
-        copy = pltpu.make_async_remote_copy(
-            src_ref=pol.at[pole],
-            dst_ref=pol.at[pole],
-            send_sem=pol_send.at[d],
-            recv_sem=pol_recv.at[d],
-            device_id={"pole": (pole + d) % n_pole},
-            device_id_type=MESH,
-        )
-        copy.start()
-        pols.append(copy)
+    total = red[at_slot(OWN)]
+    for slot in (YNZ, YPZ, YF, YFZ):
+        total = total + red[at_slot(slot)]
+    pol[pole] = weight_ref[0] * (diag_ref[...] + jnp.sum(total, axis=0, keepdims=True))
+    for d in far_first:
+        if d > 0:
+            pltpu.make_async_remote_copy(
+                src_ref=pol.at[pole],
+                dst_ref=pol.at[pole],
+                send_sem=end_send.at[1],
+                recv_sem=end_recv.at[1],
+                device_id={"pole": (pole + d) % n_pole},
+                device_id_type=MESH,
+            ).start()
 
     for slot in (OWN, YNZ, YPZ, YF, YFZ):
         place(slot, acc[at_slot(slot)])
@@ -350,16 +366,23 @@
 
     lax.fori_loop(0, rows // 32, body, 0)
 
-    for copy in pols:
-        copy.wait_recv()
-    density = pol[0]
-    for p in range(1, n_pole):
-        density = density + pol[p]
-    density_ref[...] = density[:1]
-
-    for copies in (yu, yd, zs, xu, xd, reds, pols):
+    for copies in (yu, yd, zs, xu, xd, reds):
         for copy in copies:
             copy.wait_send()
+    for i, whole in enumerate((late, pol.at[pl.ds(0, n_pole - 1)])):
+        every = pltpu.make_async_remote_copy(
+            src_ref=whole,
+            dst_ref=whole,
+            send_sem=end_send.at[i],
+            recv_sem=end_recv.at[i],
+            device_id=core,
+            device_id_type=MESH,
+        )
+        every.wait()
+    density = jnp.zeros(density_ref.shape, F32)
+    for p in range(n_pole):
+        density = density + ((pol[p] + late[0, p]) + (late[1, p] + late[2, p]))
+    density_ref[...] = density
 
 
 def hand_over(out_ref, density_ref, out_hbm, density_hbm, sems):
@@ -401,7 +424,9 @@
             pltpu.VMEM((supernode_ids.size // width, width), jnp.int32),
             pltpu.VMEM((8, 8, width), F32),
             pltpu.VMEM((8, 8, width), F32),
-            pltpu.VMEM((8, 8, width), F32),
+            pltpu.VMEM((len(NEAR), 1, width), F32),
+            pltpu.VMEM((len(NEAR), 8, 1, width), F32),
+            pltpu.VMEM((8, 1, width), F32),
             dma((8,)),
             dma((3, links)),
             dma((3, links)),
@@ -409,8 +434,8 @@
             dma((2, len(X_UP))),
             dma((8,)),
             dma((8,)),
-            dma((8,)),
-            dma((8,)),
+            dma((2,)),
+            dma((2,)),
             pltpu.SemaphoreType.REGULAR((ROUNDS,)),
         ],
         compiler_params=pltpu.CompilerParams(

time: 105 us -> 101 us (0.962)
  Pallas kernels: 104 us -> 99.5 us
    pallas_call x1, Pallas kernels: 102 us -> 98.3 us  [per_device(): pl.pallas_call(kernel, out_shape=(pltpu.VMEM((rows, 8, width), BF16), plt...]
where the time goes in v5:
time: 101 us
  Pallas kernels  99.5 us (99%)
  between operations  1.28 us (1%)
    pallas_call x1, Pallas kernels, per_device(): pl.pallas_call(kernel, out_shape=(pltpu.VMEM((rows, 8, width), BF16), plt...  98.3 us

profile of v5, /device:TPU:1, one launch (start us, length us, event | category | flops | bytes accessed | tf_op | source)
XLA Modules:
  0.0 100.8 jit_solution(15008892592144956584)
XLA Ops:
  1.3 98.3 %shard_map.77 = (bf16[768,8,128]{2,1,0:T(8,128)(2,1)S(1)}, f32[1,128]{1,0:T(1,128)S(1)}) custom-call(bf16[1,768,1536]{2,1,0:T(8,128)(2,1)} %a_hbm.1, bf16[1,6144,128]{2,1,0:T(8,128)(2,1)} %f_hbm.1, f32[1,128]{1,0:T(1,128)} %diag_hbm.1, f32[1]{0:T(128)S(6)} %copy.9.weight_ref, s32[32,48]{1,0:T(8,128)} %bitcast.7, s32[32,128]{1,0:T(8,128)} %bitcast.8), custom_call_target="tpu_custom_call" | custom-call | flops 9663676416 | bytes 6291456 | tf_op jit(solution)/shard_map/pallas_call | solution.py:408
  99.6 1.2 %shard_map.78 = (bf16[768,8,128]{2,1,0:T(8,128)(2,1)}, f32[1,128]{1,0:T(1,128)}) custom-call(bf16[768,8,128]{2,1,0:T(8,128)(2,1)S(1)} %get-tuple-element.6.out_ref, f32[1,128]{1,0:T(1,128)S(1)} %get-tuple-element.7.density_ref), custom_call_target="tpu_custom_call" | custom-call | tf_op jit(solution)/shard_map/pallas_call | solution.py:455

commit v6 on v5

--- a/solution.py
+++ b/solution.py
@@ -418,7 +418,7 @@
             pltpu.VMEM((8, height, width), BF16),
             pltpu.VMEM((8, rows, width), F32),
             pltpu.VMEM((blocks, width), F32),
-            pltpu.VMEM((rows * 8, width), F32),
+            pltpu.VMEM((rows * 8 + 64, width), F32),
             pltpu.VMEM((1, width), F32),
             pltpu.VMEM(block_pattern.shape[::-1], jnp.int32),
             pltpu.VMEM((supernode_ids.size // width, width), jnp.int32),

time: 101 us -> 101 us (level)
  no operation moved by 1% of the time
where the time goes in v6:
time: 101 us
  Pallas kernels  99.5 us (99%)
  between operations  1.28 us (1%)
    pallas_call x1, Pallas kernels, per_device(): pl.pallas_call(kernel, out_shape=(pltpu.VMEM((rows, 8, width), BF16), plt...  98.3 us

profile of v6, /device:TPU:1, one launch (start us, length us, event | category | flops | bytes accessed | tf_op | source)
XLA Modules:
  0.0 100.8 jit_solution(14775566101103181989)
XLA Ops:
  1.3 98.3 %shard_map.77 = (bf16[768,8,128]{2,1,0:T(8,128)(2,1)S(1)}, f32[1,128]{1,0:T(1,128)S(1)}) custom-call(bf16[1,768,1536]{2,1,0:T(8,128)(2,1)} %a_hbm.1, bf16[1,6144,128]{2,1,0:T(8,128)(2,1)} %f_hbm.1, f32[1,128]{1,0:T(1,128)} %diag_hbm.1, f32[1]{0:T(128)S(6)} %copy.9.weight_ref, s32[32,48]{1,0:T(8,128)} %bitcast.7, s32[32,128]{1,0:T(8,128)} %bitcast.8), custom_call_target="tpu_custom_call" | custom-call | flops 9663676416 | bytes 6291456 | tf_op jit(solution)/shard_map/pallas_call | solution.py:408
  99.6 1.2 %shard_map.78 = (bf16[768,8,128]{2,1,0:T(8,128)(2,1)}, f32[1,128]{1,0:T(1,128)}) custom-call(bf16[768,8,128]{2,1,0:T(8,128)(2,1)S(1)} %get-tuple-element.6.out_ref, f32[1,128]{1,0:T(1,128)S(1)} %get-tuple-element.7.density_ref), custom_call_target="tpu_custom_call" | custom-call | tf_op jit(solution)/shard_map/pallas_call | solution.py:455

commit v7 on v6

--- a/solution.py
+++ b/solution.py
@@ -15,6 +15,7 @@
 YNZ, YPZ, YF, YFZ = (1, 1), (3, 1), (2, 0), (2, 1)
 SLOTS = [OWN, ZP, YN, YP, YNZ, YPZ, YF, YFZ]
 NEAR = [YP, YN, ZP]
+FAR = [YFZ, YF, YNZ, YPZ, OWN]
 
 Y_UP = [
     (OWN, YP, 0, 6), (OWN, YP, 18, 6), (OWN, YP, 12, 6), (OWN, YP, 6, 2),
@@ -36,10 +37,10 @@
     (YF, YFZ, 12, 6), (YF, YFZ, 18, 3), (YF, YFZ, 21, 3),
     (OWN, ZP, 20, 3), (OWN, ZP, 23, 1),
 ]
-HALVES = [[(0, 10), (20, 10), (40, 4)], [(10, 10), (30, 10), (44, 4)]]
+HALVES = [[(0, 11), (22, 11), (44, 2)], [(11, 11), (33, 11), (46, 2)]]
 X_UP = [(0, 3, *m) for m in HALVES[0] + HALVES[1]] + [(3, 2, *m) for m in HALVES[0]]
 X_DOWN = [(0, 1, *m) for m in HALVES[1] + HALVES[0]] + [(1, 2, *m) for m in HALVES[1]]
-CHUNKS = [(0, 20), (20, 40), (40, 48)]
+CHUNKS = [(0, 22), (22, 44), (44, 48)]
 ROUNDS = 4
 
 
@@ -206,7 +207,7 @@
                 acc[s, begin:end, :] = acc[s, begin:end, :] + term if (slot, c) in begun else term
                 begun.add((slot, c))
 
-    own_span = pl.ds(pl.multiple_of(((row * rows // depth - col + 4) % 4) * depth + (row * rows) % depth, rows), rows)
+    own_first = ((row * rows // depth - col + 4) % 4) * depth + (row * rows) % depth
     reds = []
     far_first = sorted(range(n_pole), key=lambda d: abs(d - n_pole // 2))
 
@@ -216,31 +217,48 @@
     def finish(pieces):
         totals = [acc[at_slot(slot)] + product_of([slot], first, count, slice(0, rows)) for slot, first, count in pieces]
         for (slot, _, _), total in zip(pieces, totals):
-            k, back = NEAR.index(slot), NEAR.index(((-slot[0]) % 4, slot[1]))
-            near[k] = weight_ref[0] * jnp.sum(row_sums(slot, total), axis=0, keepdims=True)
-            for d in far_first:
+            near[NEAR.index(slot)] = weight_ref[0] * jnp.sum(row_sums(slot, total, 0), axis=0, keepdims=True)
+            acc[at_slot(slot)] = total
+
+    def tell_near(distances):
+        for d in distances:
+            for slot in NEAR:
                 pltpu.make_async_remote_copy(
-                    src_ref=near.at[k],
-                    dst_ref=late.at[back, pole],
+                    src_ref=near.at[NEAR.index(slot)],
+                    dst_ref=late.at[NEAR.index(((-slot[0]) % 4, slot[1])), pole],
                     send_sem=end_send.at[0],
                     recv_sem=end_recv.at[0],
                     device_id={"pole": (pole + d) % n_pole, "row": row_of(slot)},
                     device_id_type=MESH,
                 ).start()
-        for (slot, _, _), total in zip(pieces, totals):
-            place(slot, total)
-
-    def row_sums(slot, total):
-        terms = f_all[at_slot(slot), own_span, :].astype(F32) * total
-        return jnp.sum(terms.reshape(rows // 8, 8, terms.shape[1]), axis=0)
-
-    def reduce_rows(slot, total):
+
+    def tell_poles(distances):
+        for d in distances:
+            pltpu.make_async_remote_copy(
+                src_ref=pol.at[pole],
+                dst_ref=pol.at[pole],
+                send_sem=end_send.at[1],
+                recv_sem=end_recv.at[1],
+                device_id={"pole": (pole + d) % n_pole},
+                device_id_type=MESH,
+            ).start()
+
+    def row_sums(slot, total, first):
+        count = total.shape[0]
+        span = pl.ds(pl.multiple_of(own_first + first, 16), count)
+        terms = f_all[at_slot(slot), span, :].astype(F32) * total
+        return jnp.sum(terms.reshape(count // 8, 8, terms.shape[1]), axis=0)
+
+    late_rows = CHUNKS[2][0] * part_rows
+
+    def begin_rows(slot):
+        part[at_slot(slot)] = row_sums(slot, acc[at_slot(slot), :late_rows, :], 0)
+
+    def reduce_rows(slot):
         s = at_slot(slot)
-        sums = row_sums(slot, total)
+        part[s] = part[s] + row_sums(slot, acc[s, late_rows:, :], late_rows)
         if slot == OWN:
-            red[0] = sums
             return
-        part[s] = sums
         back = at_slot(((-slot[0]) % 4, slot[1]))
         copy = pltpu.make_async_remote_copy(
             src_ref=part.at[s],
@@ -322,11 +340,13 @@
     multiply([YF, YFZ], 3, 3)
     multiply([YF, YFZ], 9, 3)
     multiply([YF, YFZ], 21, 3)
+    for slot in FAR:
+        begin_rows(slot)
     arrived(xu, 8)
     arrived(xd, 8)
     multiply(SLOTS, 12, 6, (2,))
-    for slot in (YFZ, YF, YNZ, YPZ, OWN):
-        reduce_rows(slot, acc[at_slot(slot)])
+    for slot in FAR:
+        reduce_rows(slot)
     arrived(yu, 11)
     arrived(yd, 11)
     arrived(zs, 8)
@@ -338,24 +358,18 @@
     arrived(zs, 9)
     finish([(YP, 11, 1), (YN, 5, 1), (ZP, 23, 1)])
 
+    tell_near(far_first[:3])
     for copy in reds:
         copy.wait_recv()
-    total = red[at_slot(OWN)]
+    total = part[at_slot(OWN)]
     for slot in (YNZ, YPZ, YF, YFZ):
         total = total + red[at_slot(slot)]
     pol[pole] = weight_ref[0] * (diag_ref[...] + jnp.sum(total, axis=0, keepdims=True))
-    for d in far_first:
-        if d > 0:
-            pltpu.make_async_remote_copy(
-                src_ref=pol.at[pole],
-                dst_ref=pol.at[pole],
-                send_sem=end_send.at[1],
-                recv_sem=end_recv.at[1],
-                device_id={"pole": (pole + d) % n_pole},
-                device_id_type=MESH,
-            ).start()
-
-    for slot in (OWN, YNZ, YPZ, YF, YFZ):
+    tell_poles(far_first[:3])
+    tell_near(far_first[3:])
+    tell_poles(far_first[3:-1])
+
+    for slot in SLOTS:
         place(slot, acc[at_slot(slot)])
 
     def body(j, carry):
@@ -387,9 +401,9 @@
 
 def hand_over(out_ref, density_ref, out_hbm, density_hbm, sems):
     rows = out_ref.shape[0]
-    copies = [pltpu.make_async_copy(density_ref, density_hbm, sems.at[4])]
-    for i in range(4):
-        span = pl.ds(i * (rows // 4), rows // 4)
+    copies = [pltpu.make_async_copy(density_ref, density_hbm, sems.at[2])]
+    for i in range(2):
+        span = pl.ds(i * (rows // 2), rows // 2)
         copies.append(pltpu.make_async_copy(out_ref.at[span], out_hbm.at[span], sems.at[i]))
     for copy in copies:
         copy.start()
@@ -460,7 +474,7 @@
         ),
         in_specs=[vmem, vmem],
         out_specs=(anywhere, anywhere),
-        scratch_shapes=[dma((5,))],
+        scratch_shapes=[dma((3,))],
         compiler_params=pltpu.CompilerParams(vmem_limit_bytes=16 * 1024 * 1024),
     )(out, density)
     return out.reshape(1, rows, 8, 1, width), density.reshape(width)

time: 101 us -> 102 us (level)
  Pallas kernels: 99.5 us -> 101 us
    pallas_call x1, Pallas kernels: 98.3 us -> 99.6 us  [per_device(): pl.pallas_call(kernel, out_shape=(pltpu.VMEM((rows, 8, width), BF16), plt...]
where the time goes in v7:
time: 102 us
  Pallas kernels  101 us (99%)
  between operations  1.28 us (1%)
    pallas_call x1, Pallas kernels, per_device(): pl.pallas_call(kernel, out_shape=(pltpu.VMEM((rows, 8, width), BF16), plt...  99.6 us

profile of v7, /device:TPU:1, one launch (start us, length us, event | category | flops | bytes accessed | tf_op | source)
XLA Modules:
  0.0 102.1 jit_solution(11076003520692816516)
XLA Ops:
  1.3 99.6 %shard_map.77 = (bf16[768,8,128]{2,1,0:T(8,128)(2,1)S(1)}, f32[1,128]{1,0:T(1,128)S(1)}) custom-call(bf16[1,768,1536]{2,1,0:T(8,128)(2,1)} %a_hbm.1, bf16[1,6144,128]{2,1,0:T(8,128)(2,1)} %f_hbm.1, f32[1,128]{1,0:T(1,128)} %diag_hbm.1, f32[1]{0:T(128)S(6)} %copy.9.weight_ref, s32[32,48]{1,0:T(8,128)} %bitcast.7, s32[32,128]{1,0:T(8,128)} %bitcast.8), custom_call_target="tpu_custom_call" | custom-call | flops 9663676416 | bytes 6291456 | tf_op jit(solution)/shard_map/pallas_call | solution.py:422
  100.9 1.2 %shard_map.78 = (bf16[768,8,128]{2,1,0:T(8,128)(2,1)}, f32[1,128]{1,0:T(1,128)}) custom-call(bf16[768,8,128]{2,1,0:T(8,128)(2,1)S(1)} %get-tuple-element.6.out_ref, f32[1,128]{1,0:T(1,128)S(1)} %get-tuple-element.7.density_ref), custom_call_target="tpu_custom_call" | custom-call | tf_op jit(solution)/shard_map/pallas_call | solution.py:469
